TPU v7x, 512 devices: a whole 4x8x8 slice. The times are simulated.
512 devices in a mesh: inst: 128 (over y, z, core), tp: 4 (over x).
Axes of the slice: x: 4, y: 8, z: 8, core: 2. Of those that a mesh axis runs over, the one named last changes fastest.
Arguments:
- queries: bfloat16 [256, 4, 2560], P('inst', None, 'tp'), may hold values from -512 to 512
- new_keys: bfloat16 [256, 4, 512], P('inst', None, 'tp'), may hold values from -6 to 6
- new_values: bfloat16 [256, 4, 512], P('inst', None, 'tp'), may hold values from -24 to 24
- res_keys: bfloat16 [256, 512, 512], P('inst', None, 'tp'), may hold values from -6 to 6
- res_values: bfloat16 [256, 512, 512], P('inst', None, 'tp'), may hold values from -24 to 24
- lendable_keys: bfloat16 [1024, 128, 512], P('inst', None, 'tp'), may hold values from -6 to 6
- lendable_values: bfloat16 [1024, 128, 512], P('inst', None, 'tp'), may hold values from -24 to 24
- ctx_len: int32 [256], P('inst'), may hold values from 256 to 1024, as said below
- blocks: int32 [256, 4], P('inst'), may hold values from 0 to 7, as said below
- lender: int32 [128], replicated, may hold values from 0 to 127, as said below
- out_proj: bfloat16 [2560, 2560], P('tp'), may hold values from -0.625 to 0.625
Outputs:
- layer_out: bfloat16 [256, 4, 2560], P('inst', None, 'tp')
Inputs may be any that keep to these rules, and one draw needn't show every extreme that they name: The first min(ctx_len, 512) tokens of a request sit in its resident cache, the rest in ceil((ctx_len - 512) / 128) lent blocks, all full but the last; the largest value is reached. The 2 lists of one instance together name every pool slot 0 to 7 once; a request's lent blocks are the first entries of its list in order of its tokens. `lender`: a permutation of the instances that forms one cycle through all of them.
All inputs are finite; a program needn't handle non-finite values.
Results may differ from a plain program's by a relative error of at most 0.0051.
Values may be sent and summed in bfloat16 or wider, within the bound.
No kernel may reach another device: no remote copies, remote signals or barrier semaphores. Data moves between devices by JAX's collectives and lax.ppermute only.
A program may use at most 64 MiB of HBM per device.

v0:
```python
import math

import jax
import jax.numpy as jnp
from jax import lax
from jax.sharding import PartitionSpec as P

HEAD_SIZE = 128


big_negative = -1e30


def masked_max(scores, valid):
    return jnp.max(jnp.where(valid, scores, big_negative), axis=-1)


def masked_weights(scores, valid, joint_max):
    return jnp.where(
        valid, jnp.exp(jnp.where(valid, scores, big_negative) - joint_max[..., None]), 0.0
    )


def local(
    queries,
    new_keys,
    new_values,
    res_keys,
    res_values,
    lendable_keys,
    lendable_values,
    ctx_len,
    blocks,
    lender,
    out_proj,
):
    row_count, step_total, query_width = queries.shape
    key_width = res_keys.shape[2]
    kv_local = key_width // HEAD_SIZE
    group_size = query_width // key_width
    res_length = res_keys.shape[1]
    slot_count, block_len = (lendable_keys.shape[0], lendable_keys.shape[1])
    score_scale = 1.0 / math.sqrt(HEAD_SIZE)
    resident_k = res_keys.reshape(row_count, res_length, kv_local, HEAD_SIZE)
    resident_v = res_values.reshape(row_count, res_length, kv_local, HEAD_SIZE)
    fresh_k = new_keys.reshape(row_count, step_total, kv_local, HEAD_SIZE)
    fresh_v = new_values.reshape(row_count, step_total, kv_local, HEAD_SIZE)
    lent_k = lendable_keys.reshape(slot_count * block_len, kv_local, HEAD_SIZE)
    lent_v = lendable_values.reshape(slot_count * block_len, kv_local, HEAD_SIZE)
    live_res = jnp.arange(res_length)[None, :] < jnp.minimum(ctx_len, res_length)[:, None]
    list_order = jnp.arange(blocks.shape[1], dtype=jnp.int32)
    fill_counts = jnp.clip(
        ctx_len[:, None] - res_length - list_order[None, :] * block_len, 0, block_len
    )
    slot_hits = blocks[:, :, None] == jnp.arange(slot_count, dtype=jnp.int32)[None, None, :]
    fill_table = jnp.sum(jnp.where(slot_hits, fill_counts[:, :, None], 0), axis=1).astype(
        jnp.bfloat16
    )
    self_index = lax.axis_index("inst")
    inst_count = lax.axis_size("inst")
    own_lender = lender[self_index]
    borrower = jnp.sum(jnp.where(lender == self_index, jnp.arange(inst_count, dtype=jnp.int32), 0))

    def lent_attend(query_rows, table_rows, step_span):
        query_heads = query_rows.reshape(row_count, step_span, kv_local, group_size, HEAD_SIZE)
        lent_scores = (
            jnp.einsum("rsgjd,xgd->rsgjx", query_heads, lent_k, preferred_element_type=jnp.float32)
            * score_scale
        )
        lent_valid = (
            jnp.arange(block_len)[None, None, :] < table_rows.astype(jnp.float32)[:, :, None]
        )
        lent_valid = lent_valid.reshape(row_count, 1, 1, 1, slot_count * block_len)
        part_max = masked_max(lent_scores, lent_valid)
        lent_weights = masked_weights(lent_scores, lent_valid, part_max)
        part_total = jnp.sum(lent_weights, axis=-1)
        part_sum = jnp.einsum(
            "rsgjx,xgd->rsgjd",
            lent_weights.astype(jnp.bfloat16),
            lent_v,
            preferred_element_type=jnp.float32,
        )
        return (
            part_sum.reshape(row_count, -1),
            part_max.reshape(row_count, -1),
            part_total.reshape(row_count, -1),
        )

    def placed(member, target):
        empty = jnp.zeros((inst_count,) + member.shape, member.dtype)
        return lax.dynamic_update_slice_in_dim(empty, member[None], target, 0)

    def remote_part(query_sel):
        step_span = query_sel.shape[1]
        flat_query = query_sel.reshape(row_count, step_span * query_width)
        arrived = (
            lax.all_to_all(
                placed(flat_query, own_lender), "inst", split_axis=0, concat_axis=0, tiled=True
            ),
            lax.all_to_all(
                placed(fill_table, own_lender), "inst", split_axis=0, concat_axis=0, tiled=True
            ),
        )
        guest_query = lax.dynamic_index_in_dim(arrived[0], borrower, 0, keepdims=False)
        guest_table = lax.dynamic_index_in_dim(arrived[1], borrower, 0, keepdims=False)
        results = lent_attend(guest_query, guest_table, step_span)
        returned = (
            lax.all_to_all(
                placed(results[0], borrower), "inst", split_axis=0, concat_axis=0, tiled=True
            ),
            lax.all_to_all(
                placed(results[1], borrower), "inst", split_axis=0, concat_axis=0, tiled=True
            ),
            lax.all_to_all(
                placed(results[2], borrower), "inst", split_axis=0, concat_axis=0, tiled=True
            ),
        )
        results = tuple(
            (lax.dynamic_index_in_dim(member, own_lender, 0, keepdims=False) for member in returned)
        )
        remote_sum = results[0].reshape(row_count, step_span, kv_local, group_size, HEAD_SIZE)
        remote_max = results[1].reshape(row_count, step_span, kv_local, group_size)
        remote_total = results[2].reshape(row_count, step_span, kv_local, group_size)
        return (remote_max, remote_total, remote_sum)

    outputs = []
    for step_index in range(step_total):
        attend_query_sel = queries[:, step_index : step_index + 1]
        local_step_span = attend_query_sel.shape[1]
        local_query_heads = attend_query_sel.reshape(
            row_count, local_step_span, kv_local, group_size, HEAD_SIZE
        )
        res_scores = (
            jnp.einsum(
                "rsgjd,rtgd->rsgjt",
                local_query_heads,
                resident_k,
                preferred_element_type=jnp.float32,
            )
            * score_scale
        )
        new_scores = (
            jnp.einsum(
                "rsgjd,rugd->rsgju", local_query_heads, fresh_k, preferred_element_type=jnp.float32
            )
            * score_scale
        )
        res_valid = live_res[:, None, None, None, :]
        step_ids = step_index + jnp.arange(local_step_span)
        new_valid = (jnp.arange(step_total)[None, :] <= step_ids[:, None])[None, :, None, None, :]
        joint_max = jnp.maximum(
            masked_max(res_scores, res_valid), masked_max(new_scores, new_valid)
        )
        res_weights = masked_weights(res_scores, res_valid, joint_max)
        new_weights = masked_weights(new_scores, new_valid, joint_max)
        local_part_total = jnp.sum(res_weights, axis=-1) + jnp.sum(new_weights, axis=-1)
        local_part_sum = jnp.einsum(
            "rsgjt,rtgd->rsgjd",
            res_weights.astype(jnp.bfloat16),
            resident_v,
            preferred_element_type=jnp.float32,
        )
        local_part_sum = local_part_sum + jnp.einsum(
            "rsgju,rugd->rsgjd",
            new_weights.astype(jnp.bfloat16),
            fresh_v,
            preferred_element_type=jnp.float32,
        )
        attend_remote_max, attend_remote_total, attend_remote_sum = remote_part(attend_query_sel)
        attend_joint_max = jnp.maximum(joint_max, attend_remote_max)
        local_factor = jnp.exp(joint_max - attend_joint_max)
        remote_factor = jnp.exp(attend_remote_max - attend_joint_max)
        numerator = (
            local_factor[..., None] * local_part_sum + remote_factor[..., None] * attend_remote_sum
        )
        denominator = local_factor * local_part_total + remote_factor * attend_remote_total
        attend_attended = (numerator / denominator[..., None]).astype(jnp.bfloat16)
        terms = jnp.einsum(
            "rsc,co->rso",
            attend_attended.reshape(row_count, attend_query_sel.shape[1], query_width),
            out_proj,
            preferred_element_type=jnp.float32,
        )
        outputs.append(
            lax.psum_scatter(terms, "tp", scatter_dimension=2, tiled=True).astype(jnp.bfloat16)
        )
    return jnp.concatenate(outputs, axis=1)


def solution(mesh):
    in_specs = (
        P("inst", None, "tp"),
        P("inst", None, "tp"),
        P("inst", None, "tp"),
        P("inst", None, "tp"),
        P("inst", None, "tp"),
        P("inst", None, "tp"),
        P("inst", None, "tp"),
        P("inst"),
        P("inst", None),
        P(),
        P("tp", None),
    )
    out_specs = P("inst", None, "tp")
    return jax.shard_map(local, mesh=mesh, in_specs=in_specs, out_specs=out_specs, check_vma=False)
```

profile of v0, /device:TPU:1, one launch (start us, length us, event | category | flops | bytes accessed | tf_op | source)
XLA Modules:
  0.0 553.1 jit_solution(10853600991734811333)
XLA Ops:
  13.1 18.9 %all-to-all-start = ((bf16[128,2,8]{2,1,0:T(2,128)(2,1)}), bf16[128,2,8]{2,1,0:T(2,128)(2,1)}, u32[]{:S(2)}, u32[]{:S(2)}) async-start(bf16[128,2,8]{2,1,0:T(2,128)(2,1)} %constant_dynamic-update-slice_fusion.16), calls=%async_computation | async-start | bytes 131072 | tf_op jit(solution)/shard_map/all_to_all | solution.py:100
  56.2 14.1 %all-to-all-start.13 = ((bf16[128,2,640]{2,1,0:T(2,128)(2,1)}), bf16[128,2,640]{2,1,0:T(2,128)(2,1)}, u32[]{:S(2)}, u32[]{:S(2)}) async-start(bf16[128,2,640]{2,1,0:T(2,128)(2,1)} %constant_dynamic-update-slice_fusion.3), calls=%async_computation.13 | async-start | bytes 655360 | tf_op jit(solution)/shard_map/all_to_all | solution.py:97
  75.9 9.7 %all-to-all-done.13 = bf16[128,2,640]{2,1,0:T(2,128)(2,1)} async-done(((bf16[128,2,640]{2,1,0:T(2,128)(2,1)}), bf16[128,2,640]{2,1,0:T(2,128)(2,1)}, u32[]{:S(2)}, u32[]{:S(2)}) %all-to-all-start.13) | async-done | bytes 327712 | tf_op jit(solution)/shard_map/all_to_all | solution.py:97
  85.6 8.0 %all-to-all-start.1 = ((bf16[128,2,640]{2,1,0:T(2,128)(2,1)}), bf16[128,2,640]{2,1,0:T(2,128)(2,1)}, u32[]{:S(2)}, u32[]{:S(2)}) async-start(bf16[128,2,640]{2,1,0:T(2,128)(2,1)} %constant_dynamic-update-slice_fusion.15), calls=%async_computation.1 | async-start | bytes 655360 | tf_op jit(solution)/shard_map/all_to_all | solution.py:97
  97.7 11.3 %all-to-all-done.1 = bf16[128,2,640]{2,1,0:T(2,128)(2,1)} async-done(((bf16[128,2,640]{2,1,0:T(2,128)(2,1)}), bf16[128,2,640]{2,1,0:T(2,128)(2,1)}, u32[]{:S(2)}, u32[]{:S(2)}) %all-to-all-start.1) | async-done | bytes 327712 | tf_op jit(solution)/shard_map/all_to_all | solution.py:97
  109.0 8.0 %all-to-all-start.5 = ((bf16[128,2,640]{2,1,0:T(2,128)(2,1)}), bf16[128,2,640]{2,1,0:T(2,128)(2,1)}, u32[]{:S(2)}, u32[]{:S(2)}) async-start(bf16[128,2,640]{2,1,0:T(2,128)(2,1)} %constant_dynamic-update-slice_fusion.11), calls=%async_computation.5 | async-start | bytes 655360 | tf_op jit(solution)/shard_map/all_to_all | solution.py:97
  119.7 12.6 %all-to-all-done.5 = bf16[128,2,640]{2,1,0:T(2,128)(2,1)} async-done(((bf16[128,2,640]{2,1,0:T(2,128)(2,1)}), bf16[128,2,640]{2,1,0:T(2,128)(2,1)}, u32[]{:S(2)}, u32[]{:S(2)}) %all-to-all-start.5) | async-done | bytes 327712 | tf_op jit(solution)/shard_map/all_to_all | solution.py:97
  132.4 8.6 %all-to-all-start.9 = ((bf16[128,2,640]{2,1,0:T(2,128)(2,1)}), bf16[128,2,640]{2,1,0:T(2,128)(2,1)}, u32[]{:S(2)}, u32[]{:S(2)}) async-start(bf16[128,2,640]{2,1,0:T(2,128)(2,1)} %constant_dynamic-update-slice_fusion.7), calls=%async_computation.9 | async-start | bytes 655360 | tf_op jit(solution)/shard_map/all_to_all | solution.py:97
  148.7 7.7 %all-to-all-done.9 = bf16[128,2,640]{2,1,0:T(2,128)(2,1)} async-done(((bf16[128,2,640]{2,1,0:T(2,128)(2,1)}), bf16[128,2,640]{2,1,0:T(2,128)(2,1)}, u32[]{:S(2)}, u32[]{:S(2)}) %all-to-all-start.9) | async-done | bytes 327712 | tf_op jit(solution)/shard_map/all_to_all | solution.py:97
  162.5 7.8 %all-to-all-start.4 = ((f32[128,2,5]{2,1,0:T(2,128)}), f32[128,2,5]{2,1,0:T(2,128)}, u32[]{:S(2)}, u32[]{:S(2)}) async-start(f32[128,2,5]{2,1,0:T(2,128)} %constant_dynamic-update-slice_fusion.12), calls=%async_computation.4 | async-start | bytes 262144 | tf_op jit(solution)/shard_map/all_to_all | solution.py:114
  174.2 8.4 %all-to-all-done.4 = f32[128,2,5]{2,1,0:T(2,128)} async-done(((f32[128,2,5]{2,1,0:T(2,128)}), f32[128,2,5]{2,1,0:T(2,128)}, u32[]{:S(2)}, u32[]{:S(2)}) %all-to-all-start.4) | async-done | bytes 5152 | tf_op jit(solution)/shard_map/all_to_all | solution.py:114
  191.3 10.4 %all-to-all-done.2 = f32[128,2,5]{2,1,0:T(2,128)} async-done(((f32[128,2,5]{2,1,0:T(2,128)}), f32[128,2,5]{2,1,0:T(2,128)}, u32[]{:S(2)}, u32[]{:S(2)}) %all-to-all-start.2) | async-done | bytes 5152 | tf_op jit(solution)/shard_map/all_to_all | solution.py:111
  209.8 11.0 %all-to-all-done.8 = f32[128,2,5]{2,1,0:T(2,128)} async-done(((f32[128,2,5]{2,1,0:T(2,128)}), f32[128,2,5]{2,1,0:T(2,128)}, u32[]{:S(2)}, u32[]{:S(2)}) %all-to-all-start.8) | async-done | bytes 5152 | tf_op jit(solution)/shard_map/all_to_all | solution.py:114
  220.8 6.9 %all-to-all-start.6 = ((f32[128,2,5]{2,1,0:T(2,128)}), f32[128,2,5]{2,1,0:T(2,128)}, u32[]{:S(2)}, u32[]{:S(2)}) async-start(f32[128,2,5]{2,1,0:T(2,128)} %constant_dynamic-update-slice_fusion.10), calls=%async_computation.6 | async-start | bytes 262144 | tf_op jit(solution)/shard_map/all_to_all | solution.py:111
  229.6 10.4 %all-to-all-done.6 = f32[128,2,5]{2,1,0:T(2,128)} async-done(((f32[128,2,5]{2,1,0:T(2,128)}), f32[128,2,5]{2,1,0:T(2,128)}, u32[]{:S(2)}, u32[]{:S(2)}) %all-to-all-start.6) | async-done | bytes 5152 | tf_op jit(solution)/shard_map/all_to_all | solution.py:111
  248.0 11.1 %all-to-all-done.12 = f32[128,2,5]{2,1,0:T(2,128)} async-done(((f32[128,2,5]{2,1,0:T(2,128)}), f32[128,2,5]{2,1,0:T(2,128)}, u32[]{:S(2)}, u32[]{:S(2)}) %all-to-all-start.12) | async-done | bytes 5152 | tf_op jit(solution)/shard_map/all_to_all | solution.py:114
  259.1 7.0 %all-to-all-start.10 = ((f32[128,2,5]{2,1,0:T(2,128)}), f32[128,2,5]{2,1,0:T(2,128)}, u32[]{:S(2)}, u32[]{:S(2)}) async-start(f32[128,2,5]{2,1,0:T(2,128)} %constant_dynamic-update-slice_fusion.6), calls=%async_computation.10 | async-start | bytes 262144 | tf_op jit(solution)/shard_map/all_to_all | solution.py:111
  268.0 10.4 %all-to-all-done.10 = f32[128,2,5]{2,1,0:T(2,128)} async-done(((f32[128,2,5]{2,1,0:T(2,128)}), f32[128,2,5]{2,1,0:T(2,128)}, u32[]{:S(2)}, u32[]{:S(2)}) %all-to-all-start.10) | async-done | bytes 5152 | tf_op jit(solution)/shard_map/all_to_all | solution.py:111
  287.0 10.4 %all-to-all-done.16 = f32[128,2,5]{2,1,0:T(2,128)} async-done(((f32[128,2,5]{2,1,0:T(2,128)}), f32[128,2,5]{2,1,0:T(2,128)}, u32[]{:S(2)}, u32[]{:S(2)}) %all-to-all-start.16) | async-done | bytes 5152 | tf_op jit(solution)/shard_map/all_to_all | solution.py:114
  306.5 10.0 %all-to-all-done.14 = f32[128,2,5]{2,1,0:T(2,128)} async-done(((f32[128,2,5]{2,1,0:T(2,128)}), f32[128,2,5]{2,1,0:T(2,128)}, u32[]{:S(2)}, u32[]{:S(2)}) %all-to-all-start.14) | async-done | bytes 5152 | tf_op jit(solution)/shard_map/all_to_all | solution.py:111
  316.5 6.9 %all-to-all-start.3 = ((f32[128,2,640]{2,1,0:T(2,128)}), f32[128,2,640]{2,1,0:T(2,128)}, u32[]{:S(2)}, u32[]{:S(2)}) async-start(f32[128,2,640]{2,1,0:T(2,128)} %constant_dynamic-update-slice_fusion.13), calls=%async_computation.3 | async-start | bytes 1310720 | tf_op jit(solution)/shard_map/all_to_all | solution.py:108
  336.9 8.5 %all-to-all-done.3 = f32[128,2,640]{2,1,0:T(2,128)} async-done(((f32[128,2,640]{2,1,0:T(2,128)}), f32[128,2,640]{2,1,0:T(2,128)}, u32[]{:S(2)}, u32[]{:S(2)}) %all-to-all-start.3) | async-done | bytes 655392 | tf_op jit(solution)/shard_map/all_to_all | solution.py:108
  345.5 8.0 %all-to-all-start.7 = ((f32[128,2,640]{2,1,0:T(2,128)}), f32[128,2,640]{2,1,0:T(2,128)}, u32[]{:S(2)}, u32[]{:S(2)}) async-start(f32[128,2,640]{2,1,0:T(2,128)} %constant_dynamic-update-slice_fusion.9), calls=%async_computation.7 | async-start | bytes 1310720 | tf_op jit(solution)/shard_map/all_to_all | solution.py:108
  366.2 9.4 %all-to-all-done.7 = f32[128,2,640]{2,1,0:T(2,128)} async-done(((f32[128,2,640]{2,1,0:T(2,128)}), f32[128,2,640]{2,1,0:T(2,128)}, u32[]{:S(2)}, u32[]{:S(2)}) %all-to-all-start.7) | async-done | bytes 655392 | tf_op jit(solution)/shard_map/all_to_all | solution.py:108
  375.6 8.4 %all-to-all-start.11 = ((f32[128,2,640]{2,1,0:T(2,128)}), f32[128,2,640]{2,1,0:T(2,128)}, u32[]{:S(2)}, u32[]{:S(2)}) async-start(f32[128,2,640]{2,1,0:T(2,128)} %constant_dynamic-update-slice_fusion.5), calls=%async_computation.11 | async-start | bytes 1310720 | tf_op jit(solution)/shard_map/all_to_all | solution.py:108
  391.5 14.6 %all-to-all-done.11 = f32[128,2,640]{2,1,0:T(2,128)} async-done(((f32[128,2,640]{2,1,0:T(2,128)}), f32[128,2,640]{2,1,0:T(2,128)}, u32[]{:S(2)}, u32[]{:S(2)}) %all-to-all-start.11) | async-done | bytes 655392 | tf_op jit(solution)/shard_map/all_to_all | solution.py:108
  406.0 8.0 %all-to-all-start.15 = ((f32[128,2,640]{2,1,0:T(2,128)}), f32[128,2,640]{2,1,0:T(2,128)}, u32[]{:S(2)}, u32[]{:S(2)}) async-start(f32[128,2,640]{2,1,0:T(2,128)} %constant_dynamic-update-slice_fusion.1), calls=%async_computation.15 | async-start | bytes 1310720 | tf_op jit(solution)/shard_map/all_to_all | solution.py:108
  423.5 12.6 %all-to-all-done.15 = f32[128,2,640]{2,1,0:T(2,128)} async-done(((f32[128,2,640]{2,1,0:T(2,128)}), f32[128,2,640]{2,1,0:T(2,128)}, u32[]{:S(2)}, u32[]{:S(2)}) %all-to-all-start.15) | async-done | bytes 655392 | tf_op jit(solution)/shard_map/all_to_all | solution.py:108
  439.7 7.6 %reduce-scatter.13.cloned.1.call-done = f32[640,2]{1,0:T(8,128)} async-done(((f32[2560,2]{1,0:T(8,128)}), f32[640,2]{1,0:T(8,128)}) %reduce-scatter.13.cloned.1.call-update) | async-done | bytes 5136
  448.4 31.3 %reduce-scatter.15.cloned.1.call-done = f32[640,2]{1,0:T(8,128)} async-done(((f32[2560,2]{1,0:T(8,128)}), f32[640,2]{1,0:T(8,128)}) %reduce-scatter.15.cloned.1.call-update) | async-done | bytes 5136
  480.8 31.4 %reduce-scatter.17.cloned.1.call-done = f32[640,2]{1,0:T(8,128)} async-done(((f32[2560,2]{1,0:T(8,128)}), f32[640,2]{1,0:T(8,128)}) %reduce-scatter.17.cloned.1.call-update) | async-done | bytes 5136
  513.3 31.3 %reduce-scatter.19.cloned.1.call-done = f32[640,2]{1,0:T(8,128)} async-done(((f32[2560,2]{1,0:T(8,128)}), f32[640,2]{1,0:T(8,128)}) %reduce-scatter.19.cloned.1.call-update) | async-done | bytes 5136
  (199 shorter events, 154.5 us)
Async XLA Ops:
  6.5 407.6 %copy-start = (bf16[640,2560]{1,0:T(8,128)(2,1)S(1)}, bf16[640,2560]{1,0:T(8,128)(2,1)}, u32[]{:S(2)}) copy-start(bf16[640,2560]{1,0:T(8,128)(2,1)} %param.21) | copy-start | bytes 9830404
  6.5 89.1 %copy-start.1 = (bf16[2,512,128]{2,1,0:T(8,128)(2,1)S(1)}, bf16[2,512,128]{2,1,0:T(8,128)(2,1)}, u32[]{:S(2)}) copy-start(bf16[2,512,128]{2,1,0:T(8,128)(2,1)} %param.14) | copy-start | bytes 786436
  13.1 43.1 %all-to-all-start = ((bf16[128,2,8]{2,1,0:T(2,128)(2,1)}), bf16[128,2,8]{2,1,0:T(2,128)(2,1)}, u32[]{:S(2)}, u32[]{:S(2)}) async-start(bf16[128,2,8]{2,1,0:T(2,128)(2,1)} %constant_dynamic-update-slice_fusion.16), calls=%async_computation | async-start | bytes 131072 | tf_op jit(solution)/shard_map/all_to_all | solution.py:100
  51.8 65.2 %copy-start.11 = (bf16[2,5,128]{2,1,0:T(8,128)(2,1)}, bf16[2,5,128]{2,1,0:T(8,128)(2,1)S(1)}, u32[]{:S(2)}) copy-start(bf16[2,5,128]{2,1,0:T(8,128)(2,1)S(1)} %reshape.889) | copy-start | bytes 7684
  56.2 29.4 %all-to-all-start.13 = ((bf16[128,2,640]{2,1,0:T(2,128)(2,1)}), bf16[128,2,640]{2,1,0:T(2,128)(2,1)}, u32[]{:S(2)}, u32[]{:S(2)}) async-start(bf16[128,2,640]{2,1,0:T(2,128)(2,1)} %constant_dynamic-update-slice_fusion.3), calls=%async_computation.13 | async-start | bytes 655360 | tf_op jit(solution)/shard_map/all_to_all | solution.py:97
  85.6 23.4 %all-to-all-start.1 = ((bf16[128,2,640]{2,1,0:T(2,128)(2,1)}), bf16[128,2,640]{2,1,0:T(2,128)(2,1)}, u32[]{:S(2)}, u32[]{:S(2)}) async-start(bf16[128,2,640]{2,1,0:T(2,128)(2,1)} %constant_dynamic-update-slice_fusion.15), calls=%async_computation.1 | async-start | bytes 655360 | tf_op jit(solution)/shard_map/all_to_all | solution.py:97
  109.0 23.4 %all-to-all-start.5 = ((bf16[128,2,640]{2,1,0:T(2,128)(2,1)}), bf16[128,2,640]{2,1,0:T(2,128)(2,1)}, u32[]{:S(2)}, u32[]{:S(2)}) async-start(bf16[128,2,640]{2,1,0:T(2,128)(2,1)} %constant_dynamic-update-slice_fusion.11), calls=%async_computation.5 | async-start | bytes 655360 | tf_op jit(solution)/shard_map/all_to_all | solution.py:97
  132.4 24.1 %all-to-all-start.9 = ((bf16[128,2,640]{2,1,0:T(2,128)(2,1)}), bf16[128,2,640]{2,1,0:T(2,128)(2,1)}, u32[]{:S(2)}, u32[]{:S(2)}) async-start(bf16[128,2,640]{2,1,0:T(2,128)(2,1)} %constant_dynamic-update-slice_fusion.7), calls=%async_computation.9 | async-start | bytes 655360 | tf_op jit(solution)/shard_map/all_to_all | solution.py:97
  144.0 141.2 %copy-start.9 = (f32[2,5]{1,0:T(2,128)}, f32[2,5]{1,0:T(2,128)S(1)}, u32[]{:S(2)}) copy-start(f32[2,5]{1,0:T(2,128)S(1)} %get-tuple-element.39) | copy-start | bytes 124
  159.0 126.2 %copy-start.10 = (f32[2,5]{1,0:T(2,128)}, f32[2,5]{1,0:T(2,128)S(1)}, u32[]{:S(2)}) copy-start(f32[2,5]{1,0:T(2,128)S(1)} %get-tuple-element.45) | copy-start | bytes 124
  162.5 20.1 %all-to-all-start.4 = ((f32[128,2,5]{2,1,0:T(2,128)}), f32[128,2,5]{2,1,0:T(2,128)}, u32[]{:S(2)}, u32[]{:S(2)}) async-start(f32[128,2,5]{2,1,0:T(2,128)} %constant_dynamic-update-slice_fusion.12), calls=%async_computation.4 | async-start | bytes 262144 | tf_op jit(solution)/shard_map/all_to_all | solution.py:114
  182.6 19.1 %all-to-all-start.2 = ((f32[128,2,5]{2,1,0:T(2,128)}), f32[128,2,5]{2,1,0:T(2,128)}, u32[]{:S(2)}, u32[]{:S(2)}) async-start(f32[128,2,5]{2,1,0:T(2,128)} %constant_dynamic-update-slice_fusion.14), calls=%async_computation.2 | async-start | bytes 262144 | tf_op jit(solution)/shard_map/all_to_all | solution.py:111
  201.7 19.1 %all-to-all-start.8 = ((f32[128,2,5]{2,1,0:T(2,128)}), f32[128,2,5]{2,1,0:T(2,128)}, u32[]{:S(2)}, u32[]{:S(2)}) async-start(f32[128,2,5]{2,1,0:T(2,128)} %constant_dynamic-update-slice_fusion.8), calls=%async_computation.8 | async-start | bytes 262144 | tf_op jit(solution)/shard_map/all_to_all | solution.py:114
  220.8 19.2 %all-to-all-start.6 = ((f32[128,2,5]{2,1,0:T(2,128)}), f32[128,2,5]{2,1,0:T(2,128)}, u32[]{:S(2)}, u32[]{:S(2)}) async-start(f32[128,2,5]{2,1,0:T(2,128)} %constant_dynamic-update-slice_fusion.10), calls=%async_computation.6 | async-start | bytes 262144 | tf_op jit(solution)/shard_map/all_to_all | solution.py:111
  240.0 19.0 %all-to-all-start.12 = ((f32[128,2,5]{2,1,0:T(2,128)}), f32[128,2,5]{2,1,0:T(2,128)}, u32[]{:S(2)}, u32[]{:S(2)}) async-start(f32[128,2,5]{2,1,0:T(2,128)} %constant_dynamic-update-slice_fusion.4), calls=%async_computation.12 | async-start | bytes 262144 | tf_op jit(solution)/shard_map/all_to_all | solution.py:114
  259.1 19.3 %all-to-all-start.10 = ((f32[128,2,5]{2,1,0:T(2,128)}), f32[128,2,5]{2,1,0:T(2,128)}, u32[]{:S(2)}, u32[]{:S(2)}) async-start(f32[128,2,5]{2,1,0:T(2,128)} %constant_dynamic-update-slice_fusion.6), calls=%async_computation.10 | async-start | bytes 262144 | tf_op jit(solution)/shard_map/all_to_all | solution.py:111
  278.4 19.0 %all-to-all-start.16 = ((f32[128,2,5]{2,1,0:T(2,128)}), f32[128,2,5]{2,1,0:T(2,128)}, u32[]{:S(2)}, u32[]{:S(2)}) async-start(f32[128,2,5]{2,1,0:T(2,128)} %constant_dynamic-update-slice_fusion), calls=%async_computation.16 | async-start | bytes 262144 | tf_op jit(solution)/shard_map/all_to_all | solution.py:114
  297.4 19.0 %all-to-all-start.14 = ((f32[128,2,5]{2,1,0:T(2,128)}), f32[128,2,5]{2,1,0:T(2,128)}, u32[]{:S(2)}, u32[]{:S(2)}) async-start(f32[128,2,5]{2,1,0:T(2,128)} %constant_dynamic-update-slice_fusion.2), calls=%async_computation.14 | async-start | bytes 262144 | tf_op jit(solution)/shard_map/all_to_all | solution.py:111
  316.5 29.0 %all-to-all-start.3 = ((f32[128,2,640]{2,1,0:T(2,128)}), f32[128,2,640]{2,1,0:T(2,128)}, u32[]{:S(2)}, u32[]{:S(2)}) async-start(f32[128,2,640]{2,1,0:T(2,128)} %constant_dynamic-update-slice_fusion.13), calls=%async_computation.3 | async-start | bytes 1310720 | tf_op jit(solution)/shard_map/all_to_all | solution.py:108
  328.3 33.5 %copy-start.2 = (bf16[2,512,128]{2,1,0:T(8,128)(2,1)S(1)}, bf16[2,512,128]{2,1,0:T(8,128)(2,1)}, u32[]{:S(2)}) copy-start(bf16[2,512,128]{2,1,0:T(8,128)(2,1)} %param.15) | copy-start | bytes 786436
  334.6 52.3 %copy-start.5 = (f32[2,5]{1,0:T(2,128)S(1)}, f32[2,5]{1,0:T(2,128)}, u32[]{:S(2)}) copy-start(f32[2,5]{1,0:T(2,128)} %max.158) | copy-start | bytes 124
  334.6 53.0 %copy-start.4 = (f32[2,5]{1,0:T(2,128)S(1)}, f32[2,5]{1,0:T(2,128)}, u32[]{:S(2)}) copy-start(f32[2,5]{1,0:T(2,128)} %max.161) | copy-start | bytes 124
  345.5 30.2 %all-to-all-start.7 = ((f32[128,2,640]{2,1,0:T(2,128)}), f32[128,2,640]{2,1,0:T(2,128)}, u32[]{:S(2)}, u32[]{:S(2)}) async-start(f32[128,2,640]{2,1,0:T(2,128)} %constant_dynamic-update-slice_fusion.9), calls=%async_computation.7 | async-start | bytes 1310720 | tf_op jit(solution)/shard_map/all_to_all | solution.py:108
  363.4 25.7 %copy-start.20 = (f32[2,5]{1,0:T(2,128)S(1)}, f32[2,5]{1,0:T(2,128)}, u32[]{:S(2)}) copy-start(f32[2,5]{1,0:T(2,128)} %fusion.126) | copy-start | bytes 124
  363.4 27.1 %copy-start.15 = (f32[2,5,128]{2,1,0:T(8,128)S(1)}, f32[2,5,128]{2,1,0:T(8,128)}, u32[]{:S(2)}) copy-start(f32[2,5,128]{2,1,0:T(8,128)} %fusion.106) | copy-start | bytes 15364
  363.4 27.1 %copy-start.22 = (f32[2,1,1,5,4]{3,4,0,1,2:T(4,128)S(1)}, f32[2,1,1,5,4]{3,4,0,1,2:T(4,128)}, u32[]{:S(2)}) copy-start(f32[2,1,1,5,4]{3,4,0,1,2:T(4,128)} %get-tuple-element.50) | copy-start | bytes 484
  375.6 30.4 %all-to-all-start.11 = ((f32[128,2,640]{2,1,0:T(2,128)}), f32[128,2,640]{2,1,0:T(2,128)}, u32[]{:S(2)}, u32[]{:S(2)}) async-start(f32[128,2,640]{2,1,0:T(2,128)} %constant_dynamic-update-slice_fusion.5), calls=%async_computation.11 | async-start | bytes 1310720 | tf_op jit(solution)/shard_map/all_to_all | solution.py:108
  406.0 30.1 %all-to-all-start.15 = ((f32[128,2,640]{2,1,0:T(2,128)}), f32[128,2,640]{2,1,0:T(2,128)}, u32[]{:S(2)}, u32[]{:S(2)}) async-start(f32[128,2,640]{2,1,0:T(2,128)} %constant_dynamic-update-slice_fusion.1), calls=%async_computation.15 | async-start | bytes 1310720 | tf_op jit(solution)/shard_map/all_to_all | solution.py:108
  414.1 33.2 %reduce-scatter.13.cloned.1.call-start = ((), (), s32[]{:S(2)}) async-start(), calls=%async_computation.21 | async-start | bytes 1638400
  416.6 63.1 %reduce-scatter.15.cloned.1.call-start = ((), (), s32[]{:S(2)}) async-start(), calls=%async_computation.22 | async-start | bytes 1638400
  420.8 91.4 %reduce-scatter.17.cloned.1.call-start = ((), (), s32[]{:S(2)}) async-start(), calls=%async_computation.23 | async-start | bytes 1638400
  436.9 107.7 %reduce-scatter.19.cloned.1.call-start = ((), (), s32[]{:S(2)}) async-start(), calls=%async_computation.24 | async-start | bytes 1638400
  (20 other events, 210.3 us)
Sparse Core Ops, SparseCore 0:
  417.8 29.4 reduce-scatter.12
  450.1 29.5 reduce-scatter.14
  482.6 29.5 reduce-scatter.16
  514.9 29.6 reduce-scatter.18
where the time goes:
time: 564 us; the launch traced here: 553 us
  waiting for transfers between devices  270 us (48%)
  starting transfers between devices  145 us (26%)
  local copies, waits for them, and re-layouts  52.6 us (9%)
  matrix products  44.4 us (8%)
  other arithmetic  23.4 us (4%)
  between operations  17.7 us (3%)
    unnamed x8, waiting for transfers between devices  102 us
    all_to_all x4, waiting for transfers between devices, remote_part(): lax.all_to_all(placed(results[0], borrower), 'inst', split_axis=0, concat...  45.1 us
    all_to_all x4, waiting for transfers between devices, remote_part(): lax.all_to_all(placed(flat_query, own_lender), 'inst', split_axis=0, conc...  41.4 us
    all_to_all x4, waiting for transfers between devices, remote_part(): lax.all_to_all(placed(results[1], borrower), 'inst', split_axis=0, concat...  41.2 us
    all_to_all x4, waiting for transfers between devices, remote_part(): lax.all_to_all(placed(results[2], borrower), 'inst', split_axis=0, concat...  40.9 us
    all_to_all x4, starting transfers between devices, remote_part(): lax.all_to_all(placed(flat_query, own_lender), 'inst', split_axis=0, conc...  38.7 us
    all_to_all x4, starting transfers between devices, remote_part(): lax.all_to_all(placed(results[0], borrower), 'inst', split_axis=0, concat...  31.3 us
    all_to_all x4, starting transfers between devices, remote_part(): lax.all_to_all(placed(results[2], borrower), 'inst', split_axis=0, concat...  28.1 us
  transfers between devices with their start and end apart: 21, of which 20 were waited for; matrix products, arithmetic and copies ran while one was open for 19% of the time, Pallas kernels for 0%

commit v1 on v0

v1 whole, which is shorter than its diff:
```python
import functools
import math

import jax
import jax.numpy as jnp
from jax import lax
from jax.experimental import pallas as pl
from jax.experimental.pallas import tpu as pltpu
from jax.sharding import PartitionSpec as P

HEAD = 128
GROUP = 5
ROWS = 2
STEPS = 4
TILE = ROWS * STEPS
QROWS = GROUP * TILE
MSG = 48
LOW = -1e30
PARTS_M = 3
PARTS_L = 2
PER_HEAD = PARTS_M + PARTS_L
SCALE = 1.0 / math.sqrt(HEAD)
F32 = jnp.float32
BF16 = jnp.bfloat16

VMEM = pl.BlockSpec(memory_space=pltpu.VMEM)
SMEM = pl.BlockSpec(memory_space=pltpu.SMEM)


def call(kernel, outs, specs, limit=32 * 1024 * 1024):
    return pl.pallas_call(
        kernel,
        out_shape=outs,
        in_specs=specs,
        out_specs=jax.tree.map(lambda _: VMEM, outs),
        compiler_params=pltpu.CompilerParams(vmem_limit_bytes=limit),
    )


def head_rows(q_ref):
    q = jnp.concatenate([q_ref[r].astype(F32) for r in range(ROWS)], axis=0)
    return jnp.concatenate([q[:, h * HEAD : (h + 1) * HEAD] for h in range(GROUP)], axis=0)


def tile_iota(dim):
    return lax.broadcasted_iota(jnp.int32, (TILE, HEAD), dim)


def per_head(tile):
    return jnp.concatenate([tile] * GROUP, axis=0)


def pack_kernel(res_len, block_len, ctx_ref, blocks_ref, q_ref, out_ref):
    rows = head_rows(q_ref)
    side = jnp.zeros((TILE, HEAD), F32)
    request, lane = tile_iota(0) // STEPS, tile_iota(1)
    for r in range(ROWS):
        for i in range(blocks_ref.shape[1]):
            fill = jnp.clip(ctx_ref[r] - res_len - i * block_len, 0, block_len)
            hit = (request == r) & (lane == blocks_ref[r, i])
            side = jnp.where(hit, fill.astype(F32), side)
    message = jnp.concatenate([rows, side], axis=0).astype(BF16)
    for i in range(out_ref.shape[0]):
        out_ref[i] = message


def soft_part(scores, valid):
    masked = [jnp.where(v, s, LOW) for s, v in zip(scores, valid)]
    tops = [jnp.max(s, axis=1, keepdims=True) for s in masked]
    top = functools.reduce(jnp.maximum, tops)
    weights = [jnp.where(v, jnp.exp(s - top), 0.0) for s, v in zip(masked, valid)]
    total = sum(jnp.sum(w, axis=1, keepdims=True) for w in weights)
    return top, total, weights


def dot_t(a, b):
    return lax.dot_general(a, b, (((1,), (1,)), ((), ())), preferred_element_type=F32)


def home_kernel(ctx_ref, q_ref, nk_ref, nv_ref, k_ref, v_ref, o_ref, m_ref, l_ref):
    q = head_rows(q_ref).astype(BF16)
    res_len = k_ref.shape[1]
    request, step = tile_iota(0) // STEPS, tile_iota(0) % STEPS
    scores, valid = [], []
    for r in range(ROWS):
        s = dot_t(q, k_ref[r]) * SCALE
        for c in range(res_len // HEAD):
            scores.append(s[:, c * HEAD : (c + 1) * HEAD])
            valid.append(per_head((request == r) & (tile_iota(1) + c * HEAD < ctx_ref[r])))
    fill = jnp.zeros((HEAD - TILE, HEAD), F32)

    def fresh(ref):
        return jnp.concatenate([ref[r].astype(F32) for r in range(ROWS)] + [fill], axis=0)

    scores.append(dot_t(q, fresh(nk_ref).astype(BF16)) * SCALE)
    lane = tile_iota(1)
    valid.append(
        per_head((lane < TILE) & (lane // STEPS == request) & (lane % STEPS <= step))
    )
    top, total, weights = soft_part(scores, valid)
    w = [x.astype(BF16) for x in weights]
    acc = jnp.dot(w[-1], fresh(nv_ref).astype(BF16), preferred_element_type=F32)
    per = res_len // HEAD
    for r in range(ROWS):
        wide = jnp.concatenate(w[r * per : (r + 1) * per], axis=1)
        acc = acc + jnp.dot(wide, v_ref[r], preferred_element_type=F32)
    o_ref[...] = acc
    m_ref[...] = jnp.broadcast_to(top, m_ref.shape)
    l_ref[...] = jnp.broadcast_to(total, l_ref.shape)


def place_out_kernel(per_row, lender_ref, me_ref, in_ref, out_ref):
    my_row, my_col = me_ref[0] // per_row, me_ref[0] % per_row
    out_ref[...] = jnp.zeros_like(out_ref)
    for y in range(in_ref.shape[0]):
        target = lender_ref[y * per_row + my_col]

        @pl.when(target // per_row == my_row)
        def _():
            out_ref[target % per_row] = in_ref[y]


def place_back_kernel(per_row, lender_ref, me_ref, in_ref, out_ref):
    my_row, my_col = me_ref[0] // per_row, me_ref[0] % per_row
    for y in range(out_ref.shape[0]):
        source = lender_ref[y * per_row + my_col]
        mine = source // per_row == my_row

        @pl.when(mine)
        def _():
            out_ref[y] = in_ref[source % per_row]

        @pl.when(jnp.logical_not(mine))
        def _():
            out_ref[y] = jnp.zeros(out_ref.shape[1:], BF16)


def merged(in_ref):
    total = in_ref[0].astype(F32)
    for i in range(1, in_ref.shape[0]):
        total = total + in_ref[i].astype(F32)
    return total


def pieces(x, count):
    found = []
    for _ in range(count):
        piece = x.astype(BF16).astype(F32)
        found.append(piece)
        x = x - piece
    return found


def lent_kernel(in_ref, k_ref, v_ref, out_ref):
    message = merged(in_ref)
    q = message[:QROWS].astype(BF16)
    fills = message[QROWS:]
    block_len = k_ref.shape[1]
    k = k_ref[...].reshape(-1, HEAD)
    v = v_ref[...].reshape(-1, HEAD)
    s = dot_t(q, k) * SCALE
    lane = tile_iota(1).astype(F32)
    scores, valid = [], []
    for p in range(k_ref.shape[0]):
        scores.append(s[:, p * block_len : (p + 1) * block_len])
        valid.append(per_head(lane < fills[:, p : p + 1]))
    top, total, weights = soft_part(scores, valid)
    wide = jnp.concatenate([w.astype(BF16) for w in weights], axis=1)
    acc = jnp.dot(wide, v, preferred_element_type=F32)
    acc = acc * jnp.where(total > 0.0, 1.0 / jnp.maximum(total, 1e-30), 0.0)
    side = jnp.zeros((TILE, HEAD), F32)
    for h in range(GROUP):
        span = slice(h * TILE, (h + 1) * TILE)
        values = pieces(top[span], PARTS_M) + pieces(total[span], PARTS_L)
        for i, value in enumerate(values):
            side = jnp.where(tile_iota(1) == h * PER_HEAD + i, value, side)
    reply = jnp.concatenate([acc, side], axis=0).astype(BF16)
    for i in range(out_ref.shape[0]):
        out_ref[i] = reply


def project_kernel(in_ref, o_ref, m_ref, l_ref, w_ref, out_ref):
    reply = merged(in_ref)
    side = reply[QROWS:]
    heads = []
    for h in range(GROUP):
        span = slice(h * TILE, (h + 1) * TILE)
        cols = [side[:, h * PER_HEAD + i : h * PER_HEAD + i + 1] for i in range(PER_HEAD)]
        lent_top = cols[0] + cols[1] + cols[2]
        lent_total = cols[3] + cols[4]
        top = jnp.maximum(m_ref[span], lent_top)
        a = jnp.exp(m_ref[span] - top)
        b = jnp.exp(lent_top - top) * lent_total
        mixed = (a * o_ref[span] + b * reply[span]) / (a * l_ref[span] + b)
        heads.append(mixed.astype(BF16))
    attended = jnp.concatenate(heads, axis=1)
    width = out_ref.shape[2]
    for i in range(out_ref.shape[0]):
        out_ref[i] = jnp.dot(
            attended, w_ref[:, i * width : (i + 1) * width], preferred_element_type=F32
        )


def solution(mesh):
    insts, shards = mesh.shape["inst"], mesh.shape["tp"]
    per_row = 16
    lines = insts // per_row
    along_y = [[y * per_row + c for y in range(lines)] for c in range(per_row)]
    along_row = [[y * per_row + c for c in range(per_row)] for y in range(lines)]

    def exchange(x, groups):
        return lax.all_to_all(x, "inst", 0, 0, axis_index_groups=groups, tiled=True)

    def local(
        queries,
        new_keys,
        new_values,
        res_keys,
        res_values,
        lendable_keys,
        lendable_values,
        ctx_len,
        blocks,
        lender,
        out_proj,
    ):
        me = lax.axis_index("inst").astype(jnp.int32).reshape(1)

        def slots(n):
            return jax.ShapeDtypeStruct((n, MSG, HEAD), BF16)

        pack = functools.partial(pack_kernel, res_keys.shape[1], lendable_keys.shape[1])
        sent = call(pack, slots(lines), [SMEM, SMEM, VMEM])(ctx_len, blocks, queries)
        held = exchange(sent, along_y)
        part = jax.ShapeDtypeStruct((QROWS, HEAD), F32)
        home = call(home_kernel, (part, part, part), [SMEM] + [VMEM] * 5)(
            ctx_len, queries, new_keys, new_values, res_keys, res_values
        )
        place_out = functools.partial(place_out_kernel, per_row)
        placed = call(place_out, slots(per_row), [SMEM, SMEM, VMEM])(lender, me, held)
        arrived = exchange(placed, along_row)
        reply = call(lent_kernel, slots(per_row), [VMEM] * 3)(
            arrived, lendable_keys, lendable_values
        )
        held_back = exchange(reply, along_row)
        place_back = functools.partial(place_back_kernel, per_row)
        placed_back = call(place_back, slots(lines), [SMEM, SMEM, VMEM])(lender, me, held_back)
        returned = exchange(placed_back, along_y)
        width = out_proj.shape[1] // shards
        terms = call(
            project_kernel,
            jax.ShapeDtypeStruct((shards, TILE, width), F32),
            [VMEM] * 5,
        )(returned, *home, out_proj)
        shares = lax.all_to_all(terms, "tp", 0, 0, tiled=True)
        return jnp.sum(shares, axis=0).astype(BF16).reshape(ROWS, STEPS, width)

    in_specs = (
        P("inst", None, "tp"),
        P("inst", None, "tp"),
        P("inst", None, "tp"),
        P("inst", None, "tp"),
        P("inst", None, "tp"),
        P("inst", None, "tp"),
        P("inst", None, "tp"),
        P("inst"),
        P("inst", None),
        P(),
        P("tp", None),
    )
    out_specs = P("inst", None, "tp")
    return jax.shard_map(local, mesh=mesh, in_specs=in_specs, out_specs=out_specs, check_vma=False)
```

time: 564 us -> 82.3 us (0.15); the launches traced: 553 us -> 81.6 us
  waiting for transfers between devices: 270 us -> 10.8 us
  starting transfers between devices: 145 us -> 11 us
  matrix products: 44.4 us -> 0 us
  blocking collectives: 0 us -> 43.9 us
  local copies, waits for them, and re-layouts: 52.6 us -> 10.5 us
  other arithmetic: 23.4 us -> 0.01 us
  between operations: 17.7 us -> 0.06 us
    all_to_all x17 -> x2, waiting for transfers between devices: 169 us -> 10.8 us  [exchange(): return lax.all_to_all(x, 'inst', 0, 0, axis_index_groups=groups, tiled=True)]
    all_to_all x17 -> x2, starting transfers between devices: 145 us -> 11 us  [exchange(): return lax.all_to_all(x, 'inst', 0, 0, axis_index_groups=groups, tiled=True)]
    unnamed x8 -> x0, waiting for transfers between devices: 102 us -> none
    dot_general x28 -> x0, matrix products: 44.4 us -> none  [the longest x4 9.57 us: local(): jnp.einsum('rsc,co->rso', attend_attended.reshape(row_count, attend_query...]
    all_to_all x0 -> x3, blocking collectives: none -> 43.9 us  [the longest x2 35.5 us: exchange(): return lax.all_to_all(x, 'inst', 0, 0, axis_index_groups=groups, tiled=True)]
    another operation x29 -> x0, local copies, waits for them, and re-layouts: 20.2 us -> none
    dynamic_update_slice x16 -> x0, local copies, waits for them, and re-layouts: 15.9 us -> none  [placed(): return lax.dynamic_update_slice_in_dim(empty, member[None], target, 0)]
    reduce_sum x8 -> x1, other arithmetic: 10.7 us -> 0.01 us  [local(): return jnp.sum(shares, axis=0).astype(BF16).reshape(ROWS, STEPS, width)]
  transfers between devices with their start and end apart: 21 -> 2, of which waited for: 20 -> 2; matrix products, arithmetic and copies ran while one was open for 19% -> 0% of each run, Pallas kernels for 0% -> 1%
where the time goes in v1:
time: 82.3 us; the launch traced here: 81.6 us
  blocking collectives  43.9 us (53%)
  starting transfers between devices  11 us (13%)
  waiting for transfers between devices  10.8 us (13%)
  local copies, waits for them, and re-layouts  10.5 us (13%)
  Pallas kernels  5.35 us (7%)
    all_to_all x2, blocking collectives, exchange(): return lax.all_to_all(x, 'inst', 0, 0, axis_index_groups=groups, tiled=True)  35.5 us
    all_to_all x2, starting transfers between devices, exchange(): return lax.all_to_all(x, 'inst', 0, 0, axis_index_groups=groups, tiled=True)  11 us
    all_to_all x2, waiting for transfers between devices, exchange(): return lax.all_to_all(x, 'inst', 0, 0, axis_index_groups=groups, tiled=True)  10.8 us
    unnamed x28, local copies, waits for them, and re-layouts  9.86 us
    all_to_all x1, blocking collectives, local(): shares = lax.all_to_all(terms, 'tp', 0, 0, tiled=True)  8.38 us
  transfers between devices with their start and end apart: 2, of which 2 were waited for; matrix products, arithmetic and copies ran while one was open for 0% of the time, Pallas kernels for 1%

profile of v1, /device:TPU:1, one launch (start us, length us, event | category | flops | bytes accessed | tf_op | source)
XLA Modules:
  0.0 81.6 jit_solution(17679652276843645112)
XLA Ops:
  0.0 0.0 copy-start.5
  0.0 0.7 copy-done.5
  0.7 0.0 copy-start.7
  0.7 0.7 copy-done.7
  1.4 0.7 copy-done.13
  2.0 0.0 copy-start
  2.0 1.2 %shard_map.109 = bf16[8,48,128]{2,1,0:T(8,128)(2,1)} custom-call(s32[2]{0:T(128)S(1)} %copy-done.7, s32[2,4]{1,0:T(2,128)S(1)} %copy-done.13, bf16[2,4,640]{2,1,0:T(4,128)(2,1)S(1)} %copy-done.5), custom_call_target="tpu_custom_call" | custom-call | tf_op jit(solution)/shard_map/pallas_call | solution.py:233
  3.3 7.7 %all-to-all-start = ((bf16[8,48,128]{2,1,0:T(8,128)(2,1)}), bf16[8,48,128]{2,1,0:T(8,128)(2,1)S(1)}, u32[]{:S(2)}, u32[]{:S(2)}) async-start(bf16[8,48,128]{2,1,0:T(8,128)(2,1)} %shard_map.109), calls=%async_computation | async-start | bytes 196608 | tf_op jit(solution)/shard_map/all_to_all | solution.py:212
  10.9 7.6 %all-to-all-done.in_ref = bf16[8,48,128]{2,1,0:T(8,128)(2,1)S(1)} async-done(((bf16[8,48,128]{2,1,0:T(8,128)(2,1)}), bf16[8,48,128]{2,1,0:T(8,128)(2,1)S(1)}, u32[]{:S(2)}, u32[]{:S(2)}) %all-to-all-start) | async-done | bytes 98336 | tf_op jit(solution)/shard_map/all_to_all | solution.py:212
  18.5 0.7 copy-done.11
  19.1 0.7 shard_map.110
  19.8 22.6 %all_to_all.25.in_ref = bf16[16,48,128]{2,1,0:T(8,128)(2,1)S(1)} all-to-all(bf16[16,48,128]{2,1,0:T(8,128)(2,1)S(1)} %shard_map.110), channel_id=1, replica_groups={{0,4,8,12,16,20,24,28,32,36,40,44,48,52,56,60},{64,68,72,76,80,84,88,92..., dimensions={0} | all-to-all | bytes 393216 | tf_op jit(solution)/shard_map/all_to_all | solution.py:212
  42.4 0.9 %copy-done.1 = bf16[8,128,128]{2,1,0:T(8,128)(2,1)S(1)} copy-done((bf16[8,128,128]{2,1,0:T(8,128)(2,1)S(1)}, bf16[8,128,128]{2,1,0:T(8,128)(2,1)}, u32[]{:S(2)}) %copy-start.1) | copy-done | bytes 262168
  43.3 0.9 %copy-done.2 = bf16[8,128,128]{2,1,0:T(8,128)(2,1)S(1)} copy-done((bf16[8,128,128]{2,1,0:T(8,128)(2,1)S(1)}, bf16[8,128,128]{2,1,0:T(8,128)(2,1)}, u32[]{:S(2)}) %copy-start.2) | copy-done | bytes 262168
  44.3 0.4 shard_map.111
  44.7 13.0 %all_to_all.26.in_ref = bf16[16,48,128]{2,1,0:T(8,128)(2,1)S(1)} all-to-all(bf16[16,48,128]{2,1,0:T(8,128)(2,1)S(1)} %shard_map.111), channel_id=1, replica_groups={{0,4,8,12,16,20,24,28,32,36,40,44,48,52,56,60},{64,68,72,76,80,84,88,92..., dimensions={0} | all-to-all | bytes 393216 | tf_op jit(solution)/shard_map/all_to_all | solution.py:212
  57.7 0.7 copy-done.12
  58.4 1.3 %shard_map.112 = bf16[8,48,128]{2,1,0:T(8,128)(2,1)} custom-call(s32[128]{0:T(128)S(1)} %copy-done.12, s32[1]{0:T(128)} %bitcast.me_ref, bf16[16,48,128]{2,1,0:T(8,128)(2,1)S(1)} %all_to_all.26.in_ref), custom_call_target="tpu_custom_call" | custom-call | tf_op jit(solution)/shard_map/pallas_call | solution.py:247
  59.7 3.4 %all-to-all-start.3 = ((bf16[8,48,128]{2,1,0:T(8,128)(2,1)}), bf16[8,48,128]{2,1,0:T(8,128)(2,1)S(1)}, u32[]{:S(2)}, u32[]{:S(2)}) async-start(bf16[8,48,128]{2,1,0:T(8,128)(2,1)} %shard_map.112), calls=%async_computation.3 | async-start | bytes 196608 | tf_op jit(solution)/shard_map/all_to_all | solution.py:212
  63.1 0.0 copy-start.3
  63.1 0.9 %copy-done.3 = bf16[2,512,128]{2,1,0:T(8,128)(2,1)S(1)} copy-done((bf16[2,512,128]{2,1,0:T(8,128)(2,1)S(1)}, bf16[2,512,128]{2,1,0:T(8,128)(2,1)}, u32[]{:S(2)}) %copy-start.3) | copy-done | bytes 262168
  64.0 0.9 %copy-done.4 = bf16[2,512,128]{2,1,0:T(8,128)(2,1)S(1)} copy-done((bf16[2,512,128]{2,1,0:T(8,128)(2,1)S(1)}, bf16[2,512,128]{2,1,0:T(8,128)(2,1)}, u32[]{:S(2)}) %copy-start.4) | copy-done | bytes 262168
  65.0 0.7 copy-done.6
  65.7 0.7 copy-done.8
  66.3 0.7 copy-done.9
  67.0 0.7 copy-done.10
  67.7 1.0 %shard_map.113 = (f32[40,128]{1,0:T(8,128)S(1)}, f32[40,128]{1,0:T(8,128)S(1)}, f32[40,128]{1,0:T(8,128)S(1)}) custom-call(s32[2]{0:T(128)S(1)} %copy-done.8, bf16[2,4,640]{2,1,0:T(4,128)(2,1)S(1)} %copy-done.6, bf16[2,4,128]{2,1,0:T(4,128)(2,1)S(1)} %copy-done.9, bf16[2,4,128]{2,1,0:T(4,128)(2,1)S(1)} %copy-done.10, bf16[2,512,128]{2,1,0:T(8,128)(2,1)S(1)} %copy-done.3, ...), custom_call_target="tpu_custom_call" | custom-call | tf_op jit(solution)/shard_map/pallas_call | solution.py:236
  68.7 3.2 %all-to-all-done.3.in_ref = bf16[8,48,128]{2,1,0:T(8,128)(2,1)S(1)} async-done(((bf16[8,48,128]{2,1,0:T(8,128)(2,1)}), bf16[8,48,128]{2,1,0:T(8,128)(2,1)S(1)}, u32[]{:S(2)}, u32[]{:S(2)}) %all-to-all-start.3) | async-done | bytes 98336 | tf_op jit(solution)/shard_map/all_to_all | solution.py:212
  71.9 0.0 copy-done
  71.9 0.7 shard_map.114
  72.6 8.4 %all_to_all.27 = f32[4,8,640]{2,1,0:T(8,128)S(1)} all-to-all(f32[4,8,640]{2,1,0:T(8,128)S(1)} %shard_map.114), channel_id=1, replica_groups=mesh['inst'=128,'tp'=4] {'tp'}, dimensions={0} | all-to-all | bytes 163840 | tf_op jit(solution)/shard_map/all_to_all | solution.py:255
  81.0 0.6 convert_element_type.8
  (11 shorter events, 0.0 us)
Async XLA Ops:
  0.0 0.7 copy-start.5
  0.7 0.7 copy-start.7
  1.4 0.7 copy-start.13
  2.0 69.9 %copy-start = (bf16[640,2560]{1,0:T(8,128)(2,1)S(1)}, bf16[640,2560]{1,0:T(8,128)(2,1)}, u32[]{:S(2)}) copy-start(bf16[640,2560]{1,0:T(8,128)(2,1)} %w_ref.1) | copy-start | bytes 9830404
  3.3 15.2 %all-to-all-start = ((bf16[8,48,128]{2,1,0:T(8,128)(2,1)}), bf16[8,48,128]{2,1,0:T(8,128)(2,1)S(1)}, u32[]{:S(2)}, u32[]{:S(2)}) async-start(bf16[8,48,128]{2,1,0:T(8,128)(2,1)} %shard_map.109), calls=%async_computation | async-start | bytes 196608 | tf_op jit(solution)/shard_map/all_to_all | solution.py:212
  18.5 0.7 copy-start.11
  42.4 1.0 %copy-start.1 = (bf16[8,128,128]{2,1,0:T(8,128)(2,1)S(1)}, bf16[8,128,128]{2,1,0:T(8,128)(2,1)}, u32[]{:S(2)}) copy-start(bf16[8,128,128]{2,1,0:T(8,128)(2,1)} %k_ref.2) | copy-start | bytes 786436
  43.3 0.9 %copy-start.2 = (bf16[8,128,128]{2,1,0:T(8,128)(2,1)S(1)}, bf16[8,128,128]{2,1,0:T(8,128)(2,1)}, u32[]{:S(2)}) copy-start(bf16[8,128,128]{2,1,0:T(8,128)(2,1)} %v_ref.2) | copy-start | bytes 786436
  57.7 0.7 copy-start.12
  59.7 12.2 %all-to-all-start.3 = ((bf16[8,48,128]{2,1,0:T(8,128)(2,1)}), bf16[8,48,128]{2,1,0:T(8,128)(2,1)S(1)}, u32[]{:S(2)}, u32[]{:S(2)}) async-start(bf16[8,48,128]{2,1,0:T(8,128)(2,1)} %shard_map.112), calls=%async_computation.3 | async-start | bytes 196608 | tf_op jit(solution)/shard_map/all_to_all | solution.py:212
  63.1 1.0 %copy-start.3 = (bf16[2,512,128]{2,1,0:T(8,128)(2,1)S(1)}, bf16[2,512,128]{2,1,0:T(8,128)(2,1)}, u32[]{:S(2)}) copy-start(bf16[2,512,128]{2,1,0:T(8,128)(2,1)} %k_ref.3) | copy-start | bytes 786436
  64.0 0.9 %copy-start.4 = (bf16[2,512,128]{2,1,0:T(8,128)(2,1)S(1)}, bf16[2,512,128]{2,1,0:T(8,128)(2,1)}, u32[]{:S(2)}) copy-start(bf16[2,512,128]{2,1,0:T(8,128)(2,1)} %v_ref.3) | copy-start | bytes 786436
  65.0 0.7 copy-start.6
  65.7 0.7 copy-start.8
  66.3 0.7 copy-start.9
  67.0 0.7 copy-start.10

commit v2 on v1

--- a/solution.py
+++ b/solution.py
@@ -25,14 +25,20 @@
 
 VMEM = pl.BlockSpec(memory_space=pltpu.VMEM)
 SMEM = pl.BlockSpec(memory_space=pltpu.SMEM)
-
-
-def call(kernel, outs, specs, limit=32 * 1024 * 1024):
+HBM = pl.BlockSpec(memory_space=pltpu.HBM)
+
+
+def off_chip(x):
+    return pltpu.with_memory_space_constraint(x, pltpu.HBM)
+
+
+def call(kernel, outs, specs, scratch=(), limit=32 * 1024 * 1024):
     return pl.pallas_call(
         kernel,
         out_shape=outs,
         in_specs=specs,
         out_specs=jax.tree.map(lambda _: VMEM, outs),
+        scratch_shapes=scratch,
         compiler_params=pltpu.CompilerParams(vmem_limit_bytes=limit),
     )
 
@@ -42,6 +48,13 @@
     return jnp.concatenate([q[:, h * HEAD : (h + 1) * HEAD] for h in range(GROUP)], axis=0)
 
 
+def fetch(pairs, sems):
+    copies = [pltpu.make_async_copy(s, d, sems.at[i]) for i, (s, d) in enumerate(pairs)]
+    for copy in copies:
+        copy.start()
+    return copies
+
+
 def tile_iota(dim):
     return lax.broadcasted_iota(jnp.int32, (TILE, HEAD), dim)
 
@@ -50,7 +63,12 @@
     return jnp.concatenate([tile] * GROUP, axis=0)
 
 
-def pack_kernel(res_len, block_len, ctx_ref, blocks_ref, q_ref, out_ref):
+def pack_kernel(
+    res_len, block_len, ctx_hbm, blocks_hbm, q_hbm, out_ref, ctx_ref, blocks_ref, q_ref, sems
+):
+    pairs = [(q_hbm, q_ref), (ctx_hbm, ctx_ref), (blocks_hbm, blocks_ref)]
+    for copy in fetch(pairs, sems):
+        copy.wait()
     rows = head_rows(q_ref)
     side = jnp.zeros((TILE, HEAD), F32)
     request, lane = tile_iota(0) // STEPS, tile_iota(1)
@@ -77,7 +95,43 @@
     return lax.dot_general(a, b, (((1,), (1,)), ((), ())), preferred_element_type=F32)
 
 
-def home_kernel(ctx_ref, q_ref, nk_ref, nv_ref, k_ref, v_ref, o_ref, m_ref, l_ref):
+def home_kernel(
+    ctx_hbm,
+    q_hbm,
+    nk_hbm,
+    nv_hbm,
+    k_hbm,
+    v_hbm,
+    lk_hbm,
+    lv_hbm,
+    lender_hbm,
+    o_ref,
+    m_ref,
+    l_ref,
+    lk_ref,
+    lv_ref,
+    lender_ref,
+    ctx_ref,
+    q_ref,
+    nk_ref,
+    nv_ref,
+    k_ref,
+    v_ref,
+    sems,
+):
+    pairs = [
+        (ctx_hbm, ctx_ref),
+        (q_hbm, q_ref),
+        (nk_hbm, nk_ref),
+        (k_hbm, k_ref),
+        (v_hbm, v_ref),
+        (nv_hbm, nv_ref),
+        (lender_hbm, lender_ref),
+        (lk_hbm, lk_ref),
+        (lv_hbm, lv_ref),
+    ]
+    for copy in fetch(pairs, sems):
+        copy.wait()
     q = head_rows(q_ref).astype(BF16)
     res_len = k_ref.shape[1]
     request, step = tile_iota(0) // STEPS, tile_iota(0) % STEPS
@@ -230,21 +284,38 @@
             return jax.ShapeDtypeStruct((n, MSG, HEAD), BF16)
 
         pack = functools.partial(pack_kernel, res_keys.shape[1], lendable_keys.shape[1])
-        sent = call(pack, slots(lines), [SMEM, SMEM, VMEM])(ctx_len, blocks, queries)
+        def like(x, space=pltpu.VMEM):
+            return space(x.shape, x.dtype)
+
+        def out_like(x):
+            return jax.ShapeDtypeStruct(x.shape, x.dtype)
+
+        scratch = [
+            like(ctx_len, pltpu.SMEM),
+            like(blocks, pltpu.SMEM),
+            like(queries),
+            pltpu.SemaphoreType.DMA((3,)),
+        ]
+        sent = call(pack, slots(lines), [HBM] * 3, scratch)(
+            *map(off_chip, (ctx_len, blocks, queries))
+        )
         held = exchange(sent, along_y)
         part = jax.ShapeDtypeStruct((QROWS, HEAD), F32)
-        home = call(home_kernel, (part, part, part), [SMEM] + [VMEM] * 5)(
-            ctx_len, queries, new_keys, new_values, res_keys, res_values
+        outs = (part, part, part, *map(out_like, (lendable_keys, lendable_values, lender)))
+        given = (queries, new_keys, new_values, res_keys, res_values)
+        scratch = [like(ctx_len, pltpu.SMEM), *map(like, given), pltpu.SemaphoreType.DMA((9,))]
+        *home, lent_k, lent_v, table = call(home_kernel, outs, [HBM] * 9, scratch)(
+            *map(off_chip, (ctx_len, *given, lendable_keys, lendable_values, lender))
         )
         place_out = functools.partial(place_out_kernel, per_row)
-        placed = call(place_out, slots(per_row), [SMEM, SMEM, VMEM])(lender, me, held)
+        placed = call(place_out, slots(per_row), [SMEM, SMEM, VMEM])(table, me, held)
         arrived = exchange(placed, along_row)
         reply = call(lent_kernel, slots(per_row), [VMEM] * 3)(
-            arrived, lendable_keys, lendable_values
+            arrived, lent_k, lent_v
         )
         held_back = exchange(reply, along_row)
         place_back = functools.partial(place_back_kernel, per_row)
-        placed_back = call(place_back, slots(lines), [SMEM, SMEM, VMEM])(lender, me, held_back)
+        placed_back = call(place_back, slots(lines), [SMEM, SMEM, VMEM])(table, me, held_back)
         returned = exchange(placed_back, along_y)
         width = out_proj.shape[1] // shards
         terms = call(

time: 82.3 us -> 77.5 us (0.942)
  blocking collectives: 43.9 us -> 55.2 us
  local copies, waits for them, and re-layouts: 10.5 us -> 3.9 us
  waiting for transfers between devices: 10.8 us -> 4.37 us
  starting transfers between devices: 11 us -> 7.66 us
    all_to_all x2 -> x3, blocking collectives: 35.5 us -> 46.8 us  [exchange(): return lax.all_to_all(x, 'inst', 0, 0, axis_index_groups=groups, tiled=True)]
    unnamed x28 -> x10, local copies, waits for them, and re-layouts: 9.86 us -> 3.29 us
    all_to_all x2 -> x1, waiting for transfers between devices: 10.8 us -> 4.37 us  [exchange(): return lax.all_to_all(x, 'inst', 0, 0, axis_index_groups=groups, tiled=True)]
    all_to_all x2 -> x1, starting transfers between devices: 11 us -> 7.66 us  [exchange(): return lax.all_to_all(x, 'inst', 0, 0, axis_index_groups=groups, tiled=True)]
  transfers between devices with their start and end apart: 2 -> 1, of which waited for: 2 -> 1; matrix products, arithmetic and copies ran while one was open for 0% -> 0% of each run, Pallas kernels for 1% -> 2%
where the time goes in v2:
time: 77.5 us; the launch traced here: 77.1 us
  blocking collectives  55.2 us (71%)
  starting transfers between devices  7.66 us (10%)
  Pallas kernels  5.85 us (8%)
  waiting for transfers between devices  4.37 us (6%)
  local copies, waits for them, and re-layouts  3.9 us (5%)
    all_to_all x3, blocking collectives, exchange(): return lax.all_to_all(x, 'inst', 0, 0, axis_index_groups=groups, tiled=True)  46.8 us
    all_to_all x1, blocking collectives, local(): shares = lax.all_to_all(terms, 'tp', 0, 0, tiled=True)  8.38 us
    all_to_all x1, starting transfers between devices, exchange(): return lax.all_to_all(x, 'inst', 0, 0, axis_index_groups=groups, tiled=True)  7.66 us
    all_to_all x1, waiting for transfers between devices, exchange(): return lax.all_to_all(x, 'inst', 0, 0, axis_index_groups=groups, tiled=True)  4.37 us
    unnamed x10, local copies, waits for them, and re-layouts  3.29 us
    pallas_call x1, Pallas kernels, local(): call(home_kernel, outs, [HBM] * 9, scratch)  1.81 us
  transfers between devices with their start and end apart: 1, of which 1 were waited for; matrix products, arithmetic and copies ran while one was open for 0% of the time, Pallas kernels for 2%

profile of v2, /device:TPU:1, one launch (start us, length us, event | category | flops | bytes accessed | tf_op | source)
XLA Modules:
  0.0 77.1 jit_solution(4497040235966946955)
XLA Ops:
  0.0 0.0 copy-start
  0.0 1.5 %shard_map.110 = bf16[8,48,128]{2,1,0:T(8,128)(2,1)} custom-call(s32[2]{0:T(128)} %ctx_hbm.3, s32[2,4]{1,0:T(2,128)} %blocks_hbm.1, bf16[2,4,640]{2,1,0:T(4,128)(2,1)} %q_hbm.3), custom_call_target="tpu_custom_call" | custom-call | tf_op jit(solution)/shard_map/pallas_call | solution.py:299
  1.6 7.7 %all-to-all-start = ((bf16[8,48,128]{2,1,0:T(8,128)(2,1)}), bf16[8,48,128]{2,1,0:T(8,128)(2,1)S(1)}, u32[]{:S(2)}, u32[]{:S(2)}) async-start(bf16[8,48,128]{2,1,0:T(8,128)(2,1)} %shard_map.110), calls=%async_computation | async-start | bytes 196608 | tf_op jit(solution)/shard_map/all_to_all | solution.py:266
  9.2 1.8 %shard_map.109 = (f32[40,128]{1,0:T(8,128)S(1)}, f32[40,128]{1,0:T(8,128)S(1)}, f32[40,128]{1,0:T(8,128)S(1)}, bf16[8,128,128]{2,1,0:T(8,128)(2,1)S(1)}, bf16[8,...) custom-call(s32[2]{0:T(128)} %ctx_hbm.3, bf16[2,4,640]{2,1,0:T(4,128)(2,1)} %q_hbm.3, bf16[2,4,128]{2,1,0:T(4,128)(2,1)} %nk_hbm.1, ...), custom_call_target="tpu_custom_call" | custom-call | tf_op jit(solution)/shard_map/pallas_call | solution.py:307
  11.0 0.0 copy-start.1
  11.0 0.7 copy-done.1
  11.7 0.0 copy-start.3
  11.7 0.7 copy-done.3
  12.4 4.4 %all-to-all-done.in_ref = bf16[8,48,128]{2,1,0:T(8,128)(2,1)S(1)} async-done(((bf16[8,48,128]{2,1,0:T(8,128)(2,1)}), bf16[8,48,128]{2,1,0:T(8,128)(2,1)S(1)}, u32[]{:S(2)}, u32[]{:S(2)}) %all-to-all-start) | async-done | bytes 98336 | tf_op jit(solution)/shard_map/all_to_all | solution.py:266
  16.8 0.7 shard_map.111
  17.5 22.6 %all_to_all.25.in_ref = bf16[16,48,128]{2,1,0:T(8,128)(2,1)S(1)} all-to-all(bf16[16,48,128]{2,1,0:T(8,128)(2,1)S(1)} %shard_map.111), channel_id=1, replica_groups={{0,4,8,12,16,20,24,28,32,36,40,44,48,52,56,60},{64,68,72,76,80,84,88,92..., dimensions={0} | all-to-all | bytes 393216 | tf_op jit(solution)/shard_map/all_to_all | solution.py:266
  40.0 0.0 copy-start.2
  40.0 0.9 %copy-done.2 = bf16[8,128,128]{2,1,0:T(8,128)(2,1)S(1)} copy-done((bf16[8,128,128]{2,1,0:T(8,128)(2,1)S(1)}, bf16[8,128,128]{2,1,0:T(8,128)(2,1)}, u32[]{:S(2)}) %copy-start.2) | copy-done | bytes 262168
  41.0 0.0 copy-start.4
  41.0 0.9 %copy-done.4 = bf16[8,128,128]{2,1,0:T(8,128)(2,1)S(1)} copy-done((bf16[8,128,128]{2,1,0:T(8,128)(2,1)S(1)}, bf16[8,128,128]{2,1,0:T(8,128)(2,1)}, u32[]{:S(2)}) %copy-start.4) | copy-done | bytes 262168
  41.9 0.4 shard_map.112
  42.4 13.0 %all_to_all.26.in_ref = bf16[16,48,128]{2,1,0:T(8,128)(2,1)S(1)} all-to-all(bf16[16,48,128]{2,1,0:T(8,128)(2,1)S(1)} %shard_map.112), channel_id=1, replica_groups={{0,4,8,12,16,20,24,28,32,36,40,44,48,52,56,60},{64,68,72,76,80,84,88,92..., dimensions={0} | all-to-all | bytes 393216 | tf_op jit(solution)/shard_map/all_to_all | solution.py:266
  55.4 0.7 shard_map.113
  56.1 11.3 %all_to_all.27.in_ref = bf16[8,48,128]{2,1,0:T(8,128)(2,1)S(1)} all-to-all(bf16[8,48,128]{2,1,0:T(8,128)(2,1)S(1)} %shard_map.113), channel_id=1, replica_groups={{0,64,128,192,256,320,384,448},{4,68,132,196,260,324,388,452},{8,72,136..., dimensions={0} | all-to-all | bytes 196608 | tf_op jit(solution)/shard_map/all_to_all | solution.py:266
  67.4 0.0 copy-done
  67.4 0.7 shard_map.114
  68.1 8.4 %all_to_all.28 = f32[4,8,640]{2,1,0:T(8,128)S(1)} all-to-all(f32[4,8,640]{2,1,0:T(8,128)S(1)} %shard_map.114), channel_id=1, replica_groups=mesh['inst'=128,'tp'=4] {'tp'}, dimensions={0} | all-to-all | bytes 163840 | tf_op jit(solution)/shard_map/all_to_all | solution.py:326
  76.4 0.6 convert_element_type.8
  (1 shorter events, 0.0 us)
Async XLA Ops:
  0.0 67.4 %copy-start = (bf16[640,2560]{1,0:T(8,128)(2,1)S(1)}, bf16[640,2560]{1,0:T(8,128)(2,1)}, u32[]{:S(2)}) copy-start(bf16[640,2560]{1,0:T(8,128)(2,1)} %w_ref.1) | copy-start | bytes 9830404
  1.6 15.2 %all-to-all-start = ((bf16[8,48,128]{2,1,0:T(8,128)(2,1)}), bf16[8,48,128]{2,1,0:T(8,128)(2,1)S(1)}, u32[]{:S(2)}, u32[]{:S(2)}) async-start(bf16[8,48,128]{2,1,0:T(8,128)(2,1)} %shard_map.110), calls=%async_computation | async-start | bytes 196608 | tf_op jit(solution)/shard_map/all_to_all | solution.py:266
  11.0 0.7 copy-start.1
  11.7 0.7 copy-start.3
  40.0 1.0 %copy-start.2 = (bf16[8,128,128]{2,1,0:T(8,128)(2,1)S(1)}, bf16[8,128,128]{2,1,0:T(8,128)(2,1)}, u32[]{:S(2)}) copy-start(bf16[8,128,128]{2,1,0:T(8,128)(2,1)} %copy-done.1) | copy-start | bytes 786436
  41.0 0.9 %copy-start.4 = (bf16[8,128,128]{2,1,0:T(8,128)(2,1)S(1)}, bf16[8,128,128]{2,1,0:T(8,128)(2,1)}, u32[]{:S(2)}) copy-start(bf16[8,128,128]{2,1,0:T(8,128)(2,1)} %copy-done.3) | copy-start | bytes 786436

commit v3 on v2

v3 whole, which is shorter than its diff:
```python
import functools
import math

import jax
import jax.numpy as jnp
from jax import lax
from jax.experimental import pallas as pl
from jax.experimental.pallas import tpu as pltpu
from jax.sharding import PartitionSpec as P

HEAD = 128
GROUP = 5
ROWS = 2
STEPS = 4
TILE = ROWS * STEPS
QROWS = GROUP * TILE
MSG = 48
OUTBOUND = MSG + QROWS
LOW = -1e30
PARTS_M = 3
PARTS_L = 2
PER_HEAD = PARTS_M + PARTS_L
SIDE_AT = 8
SCALE = 1.0 / math.sqrt(HEAD)
F32 = jnp.float32
BF16 = jnp.bfloat16

VMEM = pl.BlockSpec(memory_space=pltpu.VMEM)
SMEM = pl.BlockSpec(memory_space=pltpu.SMEM)
HBM = pl.BlockSpec(memory_space=pltpu.HBM)


def off_chip(x):
    return pltpu.with_memory_space_constraint(x, pltpu.HBM)


def kept(x):
    return pltpu.with_memory_space_constraint(x, pltpu.VMEM)


def KEPT(x):
    return pltpu.VMEM(x.shape, x.dtype)


def call(kernel, outs, specs, scratch=(), limit=32 * 1024 * 1024):
    return pl.pallas_call(
        kernel,
        out_shape=outs,
        in_specs=specs,
        out_specs=jax.tree.map(lambda _: VMEM, outs),
        scratch_shapes=scratch,
        compiler_params=pltpu.CompilerParams(vmem_limit_bytes=limit),
    )


def head_rows(q_ref):
    q = jnp.concatenate([q_ref[r].astype(F32) for r in range(ROWS)], axis=0)
    return jnp.concatenate([q[:, h * HEAD : (h + 1) * HEAD] for h in range(GROUP)], axis=0)


def fetch(pairs, sems):
    copies = [pltpu.make_async_copy(s, d, sems.at[i]) for i, (s, d) in enumerate(pairs)]
    for copy in copies:
        copy.start()
    return copies


def tile_iota(dim):
    return lax.broadcasted_iota(jnp.int32, (TILE, HEAD), dim)


def per_head(tile):
    return jnp.concatenate([tile] * GROUP, axis=0)


def soft_part(scores, valid):
    masked = [jnp.where(v, s, LOW) for s, v in zip(scores, valid)]
    tops = [jnp.max(s, axis=1, keepdims=True) for s in masked]
    top = functools.reduce(jnp.maximum, tops)
    weights = [jnp.where(v, jnp.exp(s - top), 0.0) for s, v in zip(masked, valid)]
    total = sum(jnp.sum(w, axis=1, keepdims=True) for w in weights)
    return top, total, weights


def dot_t(a, b):
    return lax.dot_general(a, b, (((1,), (1,)), ((), ())), preferred_element_type=F32)


def pieces(x, count):
    found = []
    for _ in range(count):
        piece = x.astype(BF16).astype(F32)
        found.append(piece)
        x = x - piece
    return found


def with_sides(side, top, total):
    for h in range(GROUP):
        span = slice(h * TILE, (h + 1) * TILE)
        values = pieces(top[span], PARTS_M) + pieces(total[span], PARTS_L)
        for i, value in enumerate(values):
            side = jnp.where(tile_iota(1) == SIDE_AT + h * PER_HEAD + i, value, side)
    return side


def sides(side, h):
    first = SIDE_AT + h * PER_HEAD
    cols = [side[:, first + i : first + i + 1] for i in range(PER_HEAD)]
    return cols[0] + cols[1] + cols[2], cols[3] + cols[4]


def home_kernel(
    ctx_hbm,
    blocks_hbm,
    q_hbm,
    nk_hbm,
    nv_hbm,
    k_hbm,
    v_hbm,
    lk_hbm,
    lv_hbm,
    lender_hbm,
    out_ref,
    lk_ref,
    lv_ref,
    lender_ref,
    ctx_ref,
    blocks_ref,
    q_ref,
    nk_ref,
    nv_ref,
    k_ref,
    v_ref,
    sems,
):
    pairs = [
        (q_hbm, q_ref),
        (k_hbm, k_ref),
        (ctx_hbm, ctx_ref),
        (blocks_hbm, blocks_ref),
        (nk_hbm, nk_ref),
        (nv_hbm, nv_ref),
        (v_hbm, v_ref),
        (lender_hbm, lender_ref),
        (lk_hbm, lk_ref),
        (lv_hbm, lv_ref),
    ]
    copies = fetch(pairs, sems)
    for copy in copies[:7]:
        copy.wait()
    rows = head_rows(q_ref)
    q = rows.astype(BF16)
    res_len, block_len = k_ref.shape[1], lk_ref.shape[1]
    request, step, lane = tile_iota(0) // STEPS, tile_iota(0) % STEPS, tile_iota(1)
    side = jnp.zeros((TILE, HEAD), F32)
    for r in range(ROWS):
        for i in range(blocks_ref.shape[1]):
            fill = jnp.clip(ctx_ref[r] - res_len - i * block_len, 0, block_len)
            hit = (request == r) & (lane == blocks_ref[r, i])
            side = jnp.where(hit, fill.astype(F32), side)
    scores, valid = [], []
    for r in range(ROWS):
        s = dot_t(q, k_ref[r]) * SCALE
        for c in range(res_len // HEAD):
            scores.append(s[:, c * HEAD : (c + 1) * HEAD])
            valid.append(per_head((request == r) & (lane + c * HEAD < ctx_ref[r])))
    blank = jnp.zeros((HEAD - TILE, HEAD), F32)

    def fresh(ref):
        return jnp.concatenate([ref[r].astype(F32) for r in range(ROWS)] + [blank], axis=0)

    scores.append(dot_t(q, fresh(nk_ref).astype(BF16)) * SCALE)
    valid.append(
        per_head((lane < TILE) & (lane // STEPS == request) & (lane % STEPS <= step))
    )
    top, total, weights = soft_part(scores, valid)
    w = [x.astype(BF16) for x in weights]
    acc = jnp.dot(w[-1], fresh(nv_ref).astype(BF16), preferred_element_type=F32)
    per = res_len // HEAD
    for r in range(ROWS):
        wide = jnp.concatenate(w[r * per : (r + 1) * per], axis=1)
        acc = acc + jnp.dot(wide, v_ref[r], preferred_element_type=F32)
    side = with_sides(side, top, total)
    message = jnp.concatenate([rows, side, acc / total], axis=0).astype(BF16)
    for i in range(out_ref.shape[0]):
        out_ref[i] = message
    for copy in copies[7:]:
        copy.wait()


def place_kernel(lender_ref, me_ref, in_ref, out_ref):
    per_row = out_ref.shape[0]
    out_ref[...] = jnp.zeros_like(out_ref)
    for y in range(in_ref.shape[0]):
        target = lender_ref[y * per_row + me_ref[1]]

        @pl.when(target // per_row == me_ref[0])
        def _():
            out_ref[target % per_row] = in_ref[y, :MSG]


def merged(in_ref):
    total = in_ref[0].astype(F32)
    for i in range(1, in_ref.shape[0]):
        total = total + in_ref[i].astype(F32)
    return total


def lent_kernel(in_ref, k_ref, v_ref, out_ref):
    message = merged(in_ref)
    q = message[:QROWS].astype(BF16)
    fills = message[QROWS:]
    block_len = k_ref.shape[1]
    k = k_ref[...].reshape(-1, HEAD)
    v = v_ref[...].reshape(-1, HEAD)
    s = dot_t(q, k) * SCALE
    lane = tile_iota(1).astype(F32)
    scores, valid = [], []
    for p in range(k_ref.shape[0]):
        scores.append(s[:, p * block_len : (p + 1) * block_len])
        valid.append(per_head(lane < fills[:, p : p + 1]))
    top, total, weights = soft_part(scores, valid)
    wide = jnp.concatenate([w.astype(BF16) for w in weights], axis=1)
    acc = jnp.dot(wide, v, preferred_element_type=F32)
    acc = acc * jnp.where(total > 0.0, 1.0 / jnp.maximum(total, 1e-30), 0.0)
    side = with_sides(jnp.zeros((TILE, HEAD), F32), top, total)
    reply = jnp.concatenate([acc, side], axis=0).astype(BF16)
    for i in range(out_ref.shape[0]):
        out_ref[i] = reply


def project_kernel(lender_ref, me_ref, held_ref, back_ref, w_ref, out_ref, mixed_ref):
    per_row, lines = back_ref.shape[0], held_ref.shape[0]
    mixed_ref[...] = jnp.zeros_like(mixed_ref)
    for y in range(lines):
        source = lender_ref[y * per_row + me_ref[1]]

        @pl.when(source // per_row == me_ref[0])
        def _():
            home = held_ref[y].astype(F32)
            lent = back_ref[source % per_row].astype(F32)
            for h in range(GROUP):
                home_top, home_total = sides(home[QROWS:MSG], h)
                lent_top, lent_total = sides(lent[QROWS:], h)
                top = jnp.maximum(home_top, lent_top)
                a = jnp.exp(home_top - top) * home_total
                b = jnp.exp(lent_top - top) * lent_total
                at = h * TILE
                part = a * home[MSG + at : MSG + at + TILE] + b * lent[at : at + TILE]
                mixed_ref[y * TILE : (y + 1) * TILE, h * HEAD : (h + 1) * HEAD] = part / (a + b)

    attended = mixed_ref[...].astype(BF16)
    width = out_ref.shape[2]
    shards = out_ref.shape[0] // lines
    for i in range(shards):
        terms = jnp.dot(
            attended, w_ref[:, i * width : (i + 1) * width], preferred_element_type=F32
        )
        for y in range(lines):
            out_ref[y * shards + i] = terms[y * TILE : (y + 1) * TILE].astype(BF16)


def total_kernel(in_ref, out_ref):
    total = merged(in_ref)
    for r in range(ROWS):
        out_ref[r] = total[r * STEPS : (r + 1) * STEPS].astype(BF16)


def solution(mesh):
    insts, shards = mesh.shape["inst"], mesh.shape["tp"]
    per_row = 16
    lines = insts // per_row
    cut = jax.sharding.Mesh(mesh.devices.reshape(lines, per_row, shards), ("line", "row", "tp"))

    def exchange(x, axes):
        return lax.all_to_all(x, axes, 0, 0, tiled=True)

    def local(
        queries,
        new_keys,
        new_values,
        res_keys,
        res_values,
        lendable_keys,
        lendable_values,
        ctx_len,
        blocks,
        lender,
        out_proj,
    ):
        me = jnp.stack([lax.axis_index("line"), lax.axis_index("row")]).astype(jnp.int32)

        def slots(n, rows=MSG, width=HEAD):
            return jax.ShapeDtypeStruct((n, rows, width), BF16)

        def like(x, space=pltpu.VMEM):
            return space(x.shape, x.dtype)

        numbers = (ctx_len, blocks)
        given = (queries, new_keys, new_values, res_keys, res_values)
        brought = (lendable_keys, lendable_values, lender)
        scratch = [
            *(like(x, pltpu.SMEM) for x in numbers),
            *map(like, given),
            pltpu.SemaphoreType.DMA((10,)),
        ]
        outs = (slots(lines, OUTBOUND), *map(KEPT, brought))
        sent, lent_k, lent_v, table = call(home_kernel, outs, [HBM] * 10, scratch)(
            *map(off_chip, (*numbers, *given, *brought))
        )
        held = exchange(sent, "line")
        placed = call(place_kernel, slots(per_row), [SMEM, SMEM, VMEM])(table, me, held)
        arrived = exchange(placed, "row")
        reply = call(lent_kernel, slots(per_row), [VMEM] * 3)(arrived, kept(lent_k), kept(lent_v))
        back = exchange(reply, "row")
        width = out_proj.shape[1] // shards
        rows, columns = lines * TILE, out_proj.shape[0]
        terms = call(
            project_kernel,
            slots(lines * shards, TILE, width),
            [SMEM, SMEM, VMEM, VMEM, VMEM],
            [pltpu.VMEM((rows, columns), F32)],
        )(table, me, held, back, out_proj)
        shares = exchange(terms, ("line", "tp"))
        return call(total_kernel, jax.ShapeDtypeStruct((ROWS, STEPS, width), BF16), [VMEM])(shares)

    by_head = P(("line", "row"), None, "tp")
    in_specs = (
        *[by_head] * 7,
        P(("line", "row")),
        P(("line", "row"), None),
        P(),
        P("tp", None),
    )
    return jax.shard_map(
        local, mesh=cut, in_specs=in_specs, out_specs=by_head, check_vma=False
    )
```

time: 77.5 us -> 79.6 us (1.027)
  waiting for transfers between devices: 4.37 us -> 8.49 us
  blocking collectives: 55.2 us -> 53.6 us
    all_to_all x1, waiting for transfers between devices: 4.37 us -> 8.49 us  [exchange(): return lax.all_to_all(x, axes, 0, 0, tiled=True)]
    all_to_all x4 -> x3, blocking collectives: 55.2 us -> 53.6 us  [exchange(): return lax.all_to_all(x, axes, 0, 0, tiled=True)]
    unnamed x10 -> x12, local copies, waits for them, and re-layouts: 3.29 us -> 3.97 us
    pallas_call x6 -> x5, Pallas kernels: 5.85 us -> 5.38 us  [the longest x1 1.8 us: local(): call(home_kernel, outs, [HBM] * 10, scratch)]
  transfers between devices with their start and end apart: 1 -> 1, of which waited for: 1 -> 1; matrix products, arithmetic and copies ran while one was open for 0% -> 0% of each run, Pallas kernels for 2% -> 0%
where the time goes in v3:
time: 79.6 us; the launch traced here: 79.2 us
  blocking collectives  53.6 us (67%)
  waiting for transfers between devices  8.49 us (11%)
  starting transfers between devices  7.65 us (10%)
  Pallas kernels  5.38 us (7%)
  local copies, waits for them, and re-layouts  3.97 us (5%)
    all_to_all x3, blocking collectives, exchange(): return lax.all_to_all(x, axes, 0, 0, tiled=True)  53.6 us
    all_to_all x1, waiting for transfers between devices, exchange(): return lax.all_to_all(x, axes, 0, 0, tiled=True)  8.49 us
    all_to_all x1, starting transfers between devices, exchange(): return lax.all_to_all(x, axes, 0, 0, tiled=True)  7.65 us
    unnamed x12, local copies, waits for them, and re-layouts  3.97 us
    pallas_call x1, Pallas kernels, local(): call(home_kernel, outs, [HBM] * 10, scratch)  1.8 us
    pallas_call x1, Pallas kernels, local(): call(project_kernel, slots(lines * shards, TILE, width), [SMEM, SMEM, VME...  1.77 us
  transfers between devices with their start and end apart: 1, of which 1 were waited for; matrix products, arithmetic and copies ran while one was open for 0% of the time, Pallas kernels for 0%

profile of v3, /device:TPU:1, one launch (start us, length us, event | category | flops | bytes accessed | tf_op | source)
XLA Modules:
  0.0 79.2 jit_solution(6408990298532477156)
XLA Ops:
  0.0 0.0 copy-start
  0.0 1.8 %shard_map.109 = (bf16[8,88,128]{2,1,0:T(8,128)(2,1)S(1)}, bf16[8,128,128]{2,1,0:T(8,128)(2,1)S(1)}, bf16[8,128,128]{2,1,0:T(8,128)(2,1)S(1)}, s32[128]{0:T(128)S(1)}) custom-call(s32[2]{0:T(128)} %ctx_hbm.1, s32[2,4]{1,0:T(2,128)} %blocks_hbm.1, bf16[2,4,640]{2,1,0:T(4,128)(2,1)} %q_hbm.1, bf16[2,4,128]{2,1,0:T(4,128)(2,1)} %nk_hbm.1, ...), custom_call_target="tpu_custom_call" | custom-call | tf_op jit(solution)/shard_map/pallas_call | solution.py:309
  1.8 0.0 copy-start.1
  1.8 0.7 copy-done.1
  2.5 0.0 copy-start.3
  2.5 0.7 copy-done.3
  3.2 0.0 copy-start.5
  3.2 0.7 copy-done.5
  3.9 7.7 %all-to-all-start = ((bf16[8,88,128]{2,1,0:T(8,128)(2,1)}), bf16[8,88,128]{2,1,0:T(8,128)(2,1)S(1)}, u32[]{:S(2)}, u32[]{:S(2)}) async-start(bf16[8,88,128]{2,1,0:T(8,128)(2,1)} %copy-done.5), calls=%async_computation | async-start | bytes 360448 | tf_op jit(solution)/shard_map/all_to_all | solution.py:277
  11.5 0.1 pad_add_fusion.me_ref
  11.6 8.5 %all-to-all-done.in_ref.held_ref = bf16[8,88,128]{2,1,0:T(8,128)(2,1)S(1)} async-done(((bf16[8,88,128]{2,1,0:T(8,128)(2,1)}), bf16[8,88,128]{2,1,0:T(8,128)(2,1)S(1)}, u32[]{:S(2)}, u32[]{:S(2)}) %all-to-all-start) | async-done | bytes 180256 | tf_op jit(solution)/shard_map/all_to_all | solution.py:277
  20.1 0.7 shard_map.110
  20.8 23.0 %all_to_all.20.in_ref = bf16[16,48,128]{2,1,0:T(8,128)(2,1)S(1)} all-to-all(bf16[16,48,128]{2,1,0:T(8,128)(2,1)S(1)} %shard_map.110), channel_id=1, replica_groups=mesh['line'=8,'row'=16,'tp'=4] {'row'}, dimensions={0} | all-to-all | bytes 393216 | tf_op jit(solution)/shard_map/all_to_all | solution.py:277
  43.8 0.0 copy-start.2
  43.8 0.9 %copy-done.2 = bf16[8,128,128]{2,1,0:T(8,128)(2,1)S(1)} copy-done((bf16[8,128,128]{2,1,0:T(8,128)(2,1)S(1)}, bf16[8,128,128]{2,1,0:T(8,128)(2,1)}, u32[]{:S(2)}) %copy-start.2) | copy-done | bytes 262168
  44.7 0.0 copy-start.4
  44.7 0.9 %copy-done.4 = bf16[8,128,128]{2,1,0:T(8,128)(2,1)S(1)} copy-done((bf16[8,128,128]{2,1,0:T(8,128)(2,1)S(1)}, bf16[8,128,128]{2,1,0:T(8,128)(2,1)}, u32[]{:S(2)}) %copy-start.4) | copy-done | bytes 262168
  45.7 0.4 shard_map.111
  46.1 13.0 %all_to_all.21.back_ref = bf16[16,48,128]{2,1,0:T(8,128)(2,1)S(1)} all-to-all(bf16[16,48,128]{2,1,0:T(8,128)(2,1)S(1)} %shard_map.111), channel_id=1, replica_groups=mesh['line'=8,'row'=16,'tp'=4] {'row'}, dimensions={0} | all-to-all | bytes 393216 | tf_op jit(solution)/shard_map/all_to_all | solution.py:277
  59.1 0.0 copy-done
  59.1 1.8 %shard_map.112 = bf16[32,8,640]{2,1,0:T(8,128)(2,1)S(1)} custom-call(s32[128]{0:T(128)S(1)} %get-tuple-element.9.lender_ref, s32[2]{0:T(128)S(1)} %pad_add_fusion.me_ref, bf16[8,88,128]{2,1,0:T(8,128)(2,1)S(1)} %all-to-all-done.in_ref.held_ref, bf16[16,48,128]{2,1,0:T(8,128)(2,1)S(1)} %all_to_all.21.back_ref, bf16[640,2560]{1,0:T(8,128)(2,1)S(1)} %copy-done), custom_call_target="tpu_custom_call" | custom-call | tf_op jit(solution)/shard_map/pallas_call | solution.py:319
  60.9 17.7 %all_to_all.22.in_ref = bf16[32,8,640]{2,1,0:T(8,128)(2,1)S(1)} all-to-all(bf16[32,8,640]{2,1,0:T(8,128)(2,1)S(1)} %shard_map.112), channel_id=1, replica_groups=mesh['line'=8,'row'=16,'tp'=4] {'line','tp'}, dimensions={0} | all-to-all | bytes 655360 | tf_op jit(solution)/shard_map/all_to_all | solution.py:277
  78.6 0.7 shard_map.113
Async XLA Ops:
  0.0 59.1 %copy-start = (bf16[640,2560]{1,0:T(8,128)(2,1)S(1)}, bf16[640,2560]{1,0:T(8,128)(2,1)}, u32[]{:S(2)}) copy-start(bf16[640,2560]{1,0:T(8,128)(2,1)} %w_ref.1) | copy-start | bytes 9830404
  1.8 0.7 copy-start.1
  2.5 0.7 copy-start.3
  3.2 0.7 copy-start.5
  3.9 16.2 %all-to-all-start = ((bf16[8,88,128]{2,1,0:T(8,128)(2,1)}), bf16[8,88,128]{2,1,0:T(8,128)(2,1)S(1)}, u32[]{:S(2)}, u32[]{:S(2)}) async-start(bf16[8,88,128]{2,1,0:T(8,128)(2,1)} %copy-done.5), calls=%async_computation | async-start | bytes 360448 | tf_op jit(solution)/shard_map/all_to_all | solution.py:277
  43.8 1.0 %copy-start.2 = (bf16[8,128,128]{2,1,0:T(8,128)(2,1)S(1)}, bf16[8,128,128]{2,1,0:T(8,128)(2,1)}, u32[]{:S(2)}) copy-start(bf16[8,128,128]{2,1,0:T(8,128)(2,1)} %copy-done.1) | copy-start | bytes 786436
  44.7 0.9 %copy-start.4 = (bf16[8,128,128]{2,1,0:T(8,128)(2,1)S(1)}, bf16[8,128,128]{2,1,0:T(8,128)(2,1)}, u32[]{:S(2)}) copy-start(bf16[8,128,128]{2,1,0:T(8,128)(2,1)} %copy-done.3) | copy-start | bytes 786436

commit v4 on v2

--- a/solution.py
+++ b/solution.py
@@ -102,14 +102,10 @@
     nv_hbm,
     k_hbm,
     v_hbm,
-    lk_hbm,
-    lv_hbm,
     lender_hbm,
     o_ref,
     m_ref,
     l_ref,
-    lk_ref,
-    lv_ref,
     lender_ref,
     ctx_ref,
     q_ref,
@@ -127,8 +123,6 @@
         (v_hbm, v_ref),
         (nv_hbm, nv_ref),
         (lender_hbm, lender_ref),
-        (lk_hbm, lk_ref),
-        (lv_hbm, lv_ref),
     ]
     for copy in fetch(pairs, sems):
         copy.wait()
@@ -163,8 +157,15 @@
     l_ref[...] = jnp.broadcast_to(total, l_ref.shape)
 
 
-def place_out_kernel(per_row, lender_ref, me_ref, in_ref, out_ref):
-    my_row, my_col = me_ref[0] // per_row, me_ref[0] % per_row
+def position(per_row):
+    me = lax.axis_index("inst")
+    return me // per_row, me % per_row
+
+
+def place_out_kernel(lender_ref, in_ref, lk_hbm, lv_hbm, out_ref, lk_ref, lv_ref, sems):
+    copies = fetch([(lk_hbm, lk_ref), (lv_hbm, lv_ref)], sems)
+    per_row = out_ref.shape[0]
+    my_row, my_col = position(per_row)
     out_ref[...] = jnp.zeros_like(out_ref)
     for y in range(in_ref.shape[0]):
         target = lender_ref[y * per_row + my_col]
@@ -173,20 +174,20 @@
         def _():
             out_ref[target % per_row] = in_ref[y]
 
-
-def place_back_kernel(per_row, lender_ref, me_ref, in_ref, out_ref):
-    my_row, my_col = me_ref[0] // per_row, me_ref[0] % per_row
+    for copy in copies:
+        copy.wait()
+
+
+def place_back_kernel(lender_ref, in_ref, out_ref):
+    per_row = in_ref.shape[0]
+    my_row, my_col = position(per_row)
+    out_ref[...] = jnp.zeros_like(out_ref)
     for y in range(out_ref.shape[0]):
         source = lender_ref[y * per_row + my_col]
-        mine = source // per_row == my_row
-
-        @pl.when(mine)
+
+        @pl.when(source // per_row == my_row)
         def _():
             out_ref[y] = in_ref[source % per_row]
-
-        @pl.when(jnp.logical_not(mine))
-        def _():
-            out_ref[y] = jnp.zeros(out_ref.shape[1:], BF16)
 
 
 def merged(in_ref):
@@ -278,8 +279,6 @@
         lender,
         out_proj,
     ):
-        me = lax.axis_index("inst").astype(jnp.int32).reshape(1)
-
         def slots(n):
             return jax.ShapeDtypeStruct((n, MSG, HEAD), BF16)
 
@@ -301,21 +300,22 @@
         )
         held = exchange(sent, along_y)
         part = jax.ShapeDtypeStruct((QROWS, HEAD), F32)
-        outs = (part, part, part, *map(out_like, (lendable_keys, lendable_values, lender)))
+        outs = (part, part, part, out_like(lender))
         given = (queries, new_keys, new_values, res_keys, res_values)
-        scratch = [like(ctx_len, pltpu.SMEM), *map(like, given), pltpu.SemaphoreType.DMA((9,))]
-        *home, lent_k, lent_v, table = call(home_kernel, outs, [HBM] * 9, scratch)(
-            *map(off_chip, (ctx_len, *given, lendable_keys, lendable_values, lender))
+        scratch = [like(ctx_len, pltpu.SMEM), *map(like, given), pltpu.SemaphoreType.DMA((7,))]
+        *home, table = call(home_kernel, outs, [HBM] * 7, scratch)(
+            *map(off_chip, (ctx_len, *given, lender))
         )
-        place_out = functools.partial(place_out_kernel, per_row)
-        placed = call(place_out, slots(per_row), [SMEM, SMEM, VMEM])(table, me, held)
+        outs = (slots(per_row), out_like(lendable_keys), out_like(lendable_values))
+        placed, lent_k, lent_v = call(
+            place_out_kernel, outs, [SMEM, VMEM, HBM, HBM], [pltpu.SemaphoreType.DMA((2,))]
+        )(table, held, off_chip(lendable_keys), off_chip(lendable_values))
         arrived = exchange(placed, along_row)
         reply = call(lent_kernel, slots(per_row), [VMEM] * 3)(
             arrived, lent_k, lent_v
         )
         held_back = exchange(reply, along_row)
-        place_back = functools.partial(place_back_kernel, per_row)
-        placed_back = call(place_back, slots(lines), [SMEM, SMEM, VMEM])(table, me, held_back)
+        placed_back = call(place_back_kernel, slots(lines), [SMEM, VMEM])(table, held_back)
         returned = exchange(placed_back, along_y)
         width = out_proj.shape[1] // shards
         terms = call(

time: 77.5 us -> 76.4 us (0.986)
  local copies, waits for them, and re-layouts: 3.9 us -> 0.61 us
  waiting for transfers between devices: 4.37 us -> 5.97 us
    unnamed x10 -> x2, local copies, waits for them, and re-layouts: 3.29 us -> 0.01 us
    all_to_all x1, waiting for transfers between devices: 4.37 us -> 5.97 us  [exchange(): return lax.all_to_all(x, 'inst', 0, 0, axis_index_groups=groups, tiled=True)]
where the time goes in v4:
time: 76.4 us; the launch traced here: 76 us
  blocking collectives  55.2 us (72%)
  starting transfers between devices  7.66 us (10%)
  Pallas kernels  6.53 us (9%)
  waiting for transfers between devices  5.97 us (8%)
    all_to_all x3, blocking collectives, exchange(): return lax.all_to_all(x, 'inst', 0, 0, axis_index_groups=groups, tiled=True)  46.8 us
    all_to_all x1, blocking collectives, local(): shares = lax.all_to_all(terms, 'tp', 0, 0, tiled=True)  8.38 us
    all_to_all x1, starting transfers between devices, exchange(): return lax.all_to_all(x, 'inst', 0, 0, axis_index_groups=groups, tiled=True)  7.66 us
    all_to_all x1, waiting for transfers between devices, exchange(): return lax.all_to_all(x, 'inst', 0, 0, axis_index_groups=groups, tiled=True)  5.97 us
    pallas_call x1, Pallas kernels, local(): call(home_kernel, outs, [HBM] * 7, scratch)  1.6 us
    pallas_call x1, Pallas kernels, local(): call(place_out_kernel, outs, [SMEM, VMEM, HBM, HBM], [pltpu.SemaphoreType...  1.59 us
    pallas_call x1, Pallas kernels, local(): call(pack, slots(lines), [HBM] * 3, scratch)  1.54 us
  transfers between devices with their start and end apart: 1, of which 1 were waited for; matrix products, arithmetic and copies ran while one was open for 0% of the time, Pallas kernels for 2%

profile of v4, /device:TPU:1, one launch (start us, length us, event | category | flops | bytes accessed | tf_op | source)
XLA Modules:
  0.0 76.0 jit_solution(5455411611300257332)
XLA Ops:
  0.0 0.0 copy-start
  0.0 1.5 %shard_map.110 = bf16[8,48,128]{2,1,0:T(8,128)(2,1)} custom-call(s32[2]{0:T(128)} %ctx_hbm.3, s32[2,4]{1,0:T(2,128)} %blocks_hbm.1, bf16[2,4,640]{2,1,0:T(4,128)(2,1)} %q_hbm.3), custom_call_target="tpu_custom_call" | custom-call | tf_op jit(solution)/shard_map/pallas_call | solution.py:298
  1.6 7.7 %all-to-all-start = ((bf16[8,48,128]{2,1,0:T(8,128)(2,1)}), bf16[8,48,128]{2,1,0:T(8,128)(2,1)S(1)}, u32[]{:S(2)}, u32[]{:S(2)}) async-start(bf16[8,48,128]{2,1,0:T(8,128)(2,1)} %shard_map.110), calls=%async_computation | async-start | bytes 196608 | tf_op jit(solution)/shard_map/all_to_all | solution.py:267
  9.2 1.6 %shard_map.109 = (f32[40,128]{1,0:T(8,128)S(1)}, f32[40,128]{1,0:T(8,128)S(1)}, f32[40,128]{1,0:T(8,128)S(1)}, s32[128]{0:T(128)S(1)}) custom-call(s32[2]{0:T(128)} %ctx_hbm.3, bf16[2,4,640]{2,1,0:T(4,128)(2,1)} %q_hbm.3, bf16[2,4,128]{2,1,0:T(4,128)(2,1)} %nk_hbm.1, bf16[2,4,128]{2,1,0:T(4,128)(2,1)} %nv_hbm.1, bf16[2,512,128]{2,1,0:T(8,128)(2,1)} %k_hbm.1, ...), custom_call_target="tpu_custom_call" | custom-call | tf_op jit(solution)/shard_map/pallas_call | solution.py:306
  10.8 6.0 %all-to-all-done.in_ref = bf16[8,48,128]{2,1,0:T(8,128)(2,1)S(1)} async-done(((bf16[8,48,128]{2,1,0:T(8,128)(2,1)}), bf16[8,48,128]{2,1,0:T(8,128)(2,1)S(1)}, u32[]{:S(2)}, u32[]{:S(2)}) %all-to-all-start) | async-done | bytes 98336 | tf_op jit(solution)/shard_map/all_to_all | solution.py:267
  16.8 1.6 %shard_map.111 = (bf16[16,48,128]{2,1,0:T(8,128)(2,1)S(1)}, bf16[8,128,128]{2,1,0:T(8,128)(2,1)S(1)}, bf16[8,128,128]{2,1,0:T(8,128)(2,1)S(1)}) custom-call(s32[128]{0:T(128)S(1)} %get-tuple-element.12.lender_ref, bf16[8,48,128]{2,1,0:T(8,128)(2,1)S(1)} %all-to-all-done.in_ref, bf16[8,128,128]{2,1,0:T(8,128)(2,1)} %lk_hbm.1, bf16[8,128,128]{2,1,0:T(8,128)(2,1)} %lv_hbm.1), custom_call_target="tpu_custom_call" | custom-call | tf_op jit(solution)/shard_map/pallas_call | solution.py:310
  18.4 22.6 %all_to_all.25.in_ref = bf16[16,48,128]{2,1,0:T(8,128)(2,1)S(1)} all-to-all(bf16[16,48,128]{2,1,0:T(8,128)(2,1)S(1)} %get-tuple-element.13), channel_id=1, replica_groups={{0,4,8,12,16,20,24,28,32,36,40,44,48,52,56,60},{64,68,72,76,80,84,88,92..., dimensions={0} | all-to-all | bytes 393216 | tf_op jit(solution)/shard_map/all_to_all | solution.py:267
  40.9 0.4 shard_map.112
  41.4 13.0 %all_to_all.26.in_ref = bf16[16,48,128]{2,1,0:T(8,128)(2,1)S(1)} all-to-all(bf16[16,48,128]{2,1,0:T(8,128)(2,1)S(1)} %shard_map.112), channel_id=1, replica_groups={{0,4,8,12,16,20,24,28,32,36,40,44,48,52,56,60},{64,68,72,76,80,84,88,92..., dimensions={0} | all-to-all | bytes 393216 | tf_op jit(solution)/shard_map/all_to_all | solution.py:267
  54.4 0.7 shard_map.113
  55.1 11.3 %all_to_all.27.in_ref = bf16[8,48,128]{2,1,0:T(8,128)(2,1)S(1)} all-to-all(bf16[8,48,128]{2,1,0:T(8,128)(2,1)S(1)} %shard_map.113), channel_id=1, replica_groups={{0,64,128,192,256,320,384,448},{4,68,132,196,260,324,388,452},{8,72,136..., dimensions={0} | all-to-all | bytes 196608 | tf_op jit(solution)/shard_map/all_to_all | solution.py:267
  66.4 0.0 copy-done
  66.4 0.7 shard_map.114
  67.0 8.4 %all_to_all.28 = f32[4,8,640]{2,1,0:T(8,128)S(1)} all-to-all(f32[4,8,640]{2,1,0:T(8,128)S(1)} %shard_map.114), channel_id=1, replica_groups=mesh['inst'=128,'tp'=4] {'tp'}, dimensions={0} | all-to-all | bytes 163840 | tf_op jit(solution)/shard_map/all_to_all | solution.py:326
  75.4 0.6 convert_element_type.8
  (1 shorter events, 0.0 us)
Async XLA Ops:
  0.0 66.4 %copy-start = (bf16[640,2560]{1,0:T(8,128)(2,1)S(1)}, bf16[640,2560]{1,0:T(8,128)(2,1)}, u32[]{:S(2)}) copy-start(bf16[640,2560]{1,0:T(8,128)(2,1)} %w_ref.1) | copy-start | bytes 9830404
  1.6 15.2 %all-to-all-start = ((bf16[8,48,128]{2,1,0:T(8,128)(2,1)}), bf16[8,48,128]{2,1,0:T(8,128)(2,1)S(1)}, u32[]{:S(2)}, u32[]{:S(2)}) async-start(bf16[8,48,128]{2,1,0:T(8,128)(2,1)} %shard_map.110), calls=%async_computation | async-start | bytes 196608 | tf_op jit(solution)/shard_map/all_to_all | solution.py:267

commit v5 on v2

--- a/solution.py
+++ b/solution.py
@@ -24,7 +24,6 @@
 BF16 = jnp.bfloat16
 
 VMEM = pl.BlockSpec(memory_space=pltpu.VMEM)
-SMEM = pl.BlockSpec(memory_space=pltpu.SMEM)
 HBM = pl.BlockSpec(memory_space=pltpu.HBM)
 
 
@@ -63,25 +62,6 @@
     return jnp.concatenate([tile] * GROUP, axis=0)
 
 
-def pack_kernel(
-    res_len, block_len, ctx_hbm, blocks_hbm, q_hbm, out_ref, ctx_ref, blocks_ref, q_ref, sems
-):
-    pairs = [(q_hbm, q_ref), (ctx_hbm, ctx_ref), (blocks_hbm, blocks_ref)]
-    for copy in fetch(pairs, sems):
-        copy.wait()
-    rows = head_rows(q_ref)
-    side = jnp.zeros((TILE, HEAD), F32)
-    request, lane = tile_iota(0) // STEPS, tile_iota(1)
-    for r in range(ROWS):
-        for i in range(blocks_ref.shape[1]):
-            fill = jnp.clip(ctx_ref[r] - res_len - i * block_len, 0, block_len)
-            hit = (request == r) & (lane == blocks_ref[r, i])
-            side = jnp.where(hit, fill.astype(F32), side)
-    message = jnp.concatenate([rows, side], axis=0).astype(BF16)
-    for i in range(out_ref.shape[0]):
-        out_ref[i] = message
-
-
 def soft_part(scores, valid):
     masked = [jnp.where(v, s, LOW) for s, v in zip(scores, valid)]
     tops = [jnp.max(s, axis=1, keepdims=True) for s in masked]
@@ -95,8 +75,10 @@
     return lax.dot_general(a, b, (((1,), (1,)), ((), ())), preferred_element_type=F32)
 
 
-def home_kernel(
+def first_kernel(
     ctx_hbm,
+    blocks_hbm,
+    lender_hbm,
     q_hbm,
     nk_hbm,
     nv_hbm,
@@ -104,14 +86,16 @@
     v_hbm,
     lk_hbm,
     lv_hbm,
-    lender_hbm,
+    out_ref,
     o_ref,
     m_ref,
     l_ref,
+    pick_ref,
     lk_ref,
     lv_ref,
+    ctx_ref,
+    blocks_ref,
     lender_ref,
-    ctx_ref,
     q_ref,
     nk_ref,
     nv_ref,
@@ -120,38 +104,67 @@
     sems,
 ):
     pairs = [
+        (q_hbm, q_ref),
+        (k_hbm, k_ref),
+        (lender_hbm, lender_ref),
         (ctx_hbm, ctx_ref),
-        (q_hbm, q_ref),
+        (blocks_hbm, blocks_ref),
         (nk_hbm, nk_ref),
-        (k_hbm, k_ref),
         (v_hbm, v_ref),
         (nv_hbm, nv_ref),
-        (lender_hbm, lender_ref),
         (lk_hbm, lk_ref),
         (lv_hbm, lv_ref),
     ]
-    for copy in fetch(pairs, sems):
+    copies = fetch(pairs, sems)
+    request, step, lane = tile_iota(0) // STEPS, tile_iota(0) % STEPS, tile_iota(1)
+
+    copies[2].wait()
+    lines = out_ref.shape[0]
+    per_row = pick_ref.shape[0] // lines
+    me = lax.axis_index("inst")
+    row, col = me // per_row, me % per_row
+    target = jnp.zeros((lines, HEAD), jnp.int32)
+    for y in range(lines):
+        here = lax.broadcasted_iota(jnp.int32, (lines, HEAD), 0) == y
+        target = jnp.where(here, lender_ref[y * per_row + col] - row * per_row, target)
+    for s in range(per_row):
+        pick_ref[s * lines : (s + 1) * lines] = jnp.where(target == s, 1.0, 0.0)
+
+    for copy in [copies[0], *copies[3:5]]:
         copy.wait()
-    q = head_rows(q_ref).astype(BF16)
-    res_len = k_ref.shape[1]
-    request, step = tile_iota(0) // STEPS, tile_iota(0) % STEPS
+    rows = head_rows(q_ref)
+    q = rows.astype(BF16)
+    res_len, block_len = k_ref.shape[1], lk_ref.shape[1]
+    side = jnp.zeros((TILE, HEAD), F32)
+    for r in range(ROWS):
+        for i in range(blocks_ref.shape[1]):
+            fill = jnp.clip(ctx_ref[r] - res_len - i * block_len, 0, block_len)
+            hit = (request == r) & (lane == blocks_ref[r, i])
+            side = jnp.where(hit, fill.astype(F32), side)
+    message = jnp.concatenate([rows, side], axis=0).astype(BF16)
+    for i in range(lines):
+        out_ref[i] = message
+
+    for copy in [copies[1], copies[5]]:
+        copy.wait()
     scores, valid = [], []
     for r in range(ROWS):
         s = dot_t(q, k_ref[r]) * SCALE
         for c in range(res_len // HEAD):
             scores.append(s[:, c * HEAD : (c + 1) * HEAD])
-            valid.append(per_head((request == r) & (tile_iota(1) + c * HEAD < ctx_ref[r])))
-    fill = jnp.zeros((HEAD - TILE, HEAD), F32)
+            valid.append(per_head((request == r) & (lane + c * HEAD < ctx_ref[r])))
+    blank = jnp.zeros((HEAD - TILE, HEAD), F32)
 
     def fresh(ref):
-        return jnp.concatenate([ref[r].astype(F32) for r in range(ROWS)] + [fill], axis=0)
+        return jnp.concatenate([ref[r].astype(F32) for r in range(ROWS)] + [blank], axis=0)
 
     scores.append(dot_t(q, fresh(nk_ref).astype(BF16)) * SCALE)
-    lane = tile_iota(1)
     valid.append(
         per_head((lane < TILE) & (lane // STEPS == request) & (lane % STEPS <= step))
     )
     top, total, weights = soft_part(scores, valid)
+    for copy in copies[6:8]:
+        copy.wait()
     w = [x.astype(BF16) for x in weights]
     acc = jnp.dot(w[-1], fresh(nv_ref).astype(BF16), preferred_element_type=F32)
     per = res_len // HEAD
@@ -161,32 +174,30 @@
     o_ref[...] = acc
     m_ref[...] = jnp.broadcast_to(top, m_ref.shape)
     l_ref[...] = jnp.broadcast_to(total, l_ref.shape)
-
-
-def place_out_kernel(per_row, lender_ref, me_ref, in_ref, out_ref):
-    my_row, my_col = me_ref[0] // per_row, me_ref[0] % per_row
-    out_ref[...] = jnp.zeros_like(out_ref)
-    for y in range(in_ref.shape[0]):
-        target = lender_ref[y * per_row + my_col]
-
-        @pl.when(target // per_row == my_row)
-        def _():
-            out_ref[target % per_row] = in_ref[y]
-
-
-def place_back_kernel(per_row, lender_ref, me_ref, in_ref, out_ref):
-    my_row, my_col = me_ref[0] // per_row, me_ref[0] % per_row
-    for y in range(out_ref.shape[0]):
-        source = lender_ref[y * per_row + my_col]
-        mine = source // per_row == my_row
-
-        @pl.when(mine)
-        def _():
-            out_ref[y] = in_ref[source % per_row]
-
-        @pl.when(jnp.logical_not(mine))
-        def _():
-            out_ref[y] = jnp.zeros(out_ref.shape[1:], BF16)
+    for copy in copies[8:]:
+        copy.wait()
+
+
+def place(pick_ref, in_ref, out_ref, place_of):
+    held = [in_ref[i].astype(F32) for i in range(in_ref.shape[0])]
+    for o in range(out_ref.shape[0]):
+        tiles = [jnp.zeros((TILE, HEAD), F32)] * (MSG // TILE)
+        for i, message in enumerate(held):
+            at = place_of(i, o)
+            mine = jnp.broadcast_to(pick_ref[at : at + 1], (TILE, HEAD)) > 0.5
+            tiles = [
+                jnp.where(mine, message[t * TILE : (t + 1) * TILE], tile)
+                for t, tile in enumerate(tiles)
+            ]
+        out_ref[o] = jnp.concatenate(tiles, axis=0).astype(BF16)
+
+
+def place_out_kernel(pick_ref, in_ref, out_ref):
+    place(pick_ref, in_ref, out_ref, lambda y, s: s * in_ref.shape[0] + y)
+
+
+def place_back_kernel(pick_ref, in_ref, out_ref):
+    place(pick_ref, in_ref, out_ref, lambda s, y: s * out_ref.shape[0] + y)
 
 
 def merged(in_ref):
@@ -278,44 +289,37 @@
         lender,
         out_proj,
     ):
-        me = lax.axis_index("inst").astype(jnp.int32).reshape(1)
-
         def slots(n):
             return jax.ShapeDtypeStruct((n, MSG, HEAD), BF16)
 
-        pack = functools.partial(pack_kernel, res_keys.shape[1], lendable_keys.shape[1])
         def like(x, space=pltpu.VMEM):
             return space(x.shape, x.dtype)
 
         def out_like(x):
             return jax.ShapeDtypeStruct(x.shape, x.dtype)
 
+        numbers = (ctx_len, blocks, lender)
+        given = (queries, new_keys, new_values, res_keys, res_values)
+        lent = (lendable_keys, lendable_values)
+        part = jax.ShapeDtypeStruct((QROWS, HEAD), F32)
+        picks = jax.ShapeDtypeStruct((insts, HEAD), F32)
+        outs = (slots(lines), part, part, part, picks, *map(out_like, lent))
         scratch = [
-            like(ctx_len, pltpu.SMEM),
-            like(blocks, pltpu.SMEM),
-            like(queries),
-            pltpu.SemaphoreType.DMA((3,)),
+            *(like(x, pltpu.SMEM) for x in numbers),
+            *map(like, given),
+            pltpu.SemaphoreType.DMA((10,)),
         ]
-        sent = call(pack, slots(lines), [HBM] * 3, scratch)(
-            *map(off_chip, (ctx_len, blocks, queries))
+        sent, *home, picked, lent_k, lent_v = call(first_kernel, outs, [HBM] * 10, scratch)(
+            *map(off_chip, (*numbers, *given, *lent))
         )
         held = exchange(sent, along_y)
-        part = jax.ShapeDtypeStruct((QROWS, HEAD), F32)
-        outs = (part, part, part, *map(out_like, (lendable_keys, lendable_values, lender)))
-        given = (queries, new_keys, new_values, res_keys, res_values)
-        scratch = [like(ctx_len, pltpu.SMEM), *map(like, given), pltpu.SemaphoreType.DMA((9,))]
-        *home, lent_k, lent_v, table = call(home_kernel, outs, [HBM] * 9, scratch)(
-            *map(off_chip, (ctx_len, *given, lendable_keys, lendable_values, lender))
-        )
-        place_out = functools.partial(place_out_kernel, per_row)
-        placed = call(place_out, slots(per_row), [SMEM, SMEM, VMEM])(table, me, held)
+        placed = call(place_out_kernel, slots(per_row), [VMEM] * 2)(picked, held)
         arrived = exchange(placed, along_row)
         reply = call(lent_kernel, slots(per_row), [VMEM] * 3)(
             arrived, lent_k, lent_v
         )
         held_back = exchange(reply, along_row)
-        place_back = functools.partial(place_back_kernel, per_row)
-        placed_back = call(place_back, slots(lines), [SMEM, SMEM, VMEM])(table, me, held_back)
+        placed_back = call(place_back_kernel, slots(lines), [VMEM] * 2)(picked, held_back)
         returned = exchange(placed_back, along_y)
         width = out_proj.shape[1] // shards
         terms = call(

time: 77.5 us -> 74.4 us (0.960)
  blocking collectives: 55.2 us -> 70.2 us
  starting transfers between devices: 7.66 us -> 0 us
  waiting for transfers between devices: 4.37 us -> 0 us
  local copies, waits for them, and re-layouts: 3.9 us -> 0.61 us
  Pallas kernels: 5.85 us -> 3.24 us
    all_to_all x3 -> x4, blocking collectives: 46.8 us -> 61.9 us  [exchange(): return lax.all_to_all(x, 'inst', 0, 0, axis_index_groups=groups, tiled=True)]
    all_to_all x1 -> x0, starting transfers between devices: 7.66 us -> none  [exchange(): return lax.all_to_all(x, 'inst', 0, 0, axis_index_groups=groups, tiled=True)]
    all_to_all x1 -> x0, waiting for transfers between devices: 4.37 us -> none  [exchange(): return lax.all_to_all(x, 'inst', 0, 0, axis_index_groups=groups, tiled=True)]
    unnamed x10 -> x2, local copies, waits for them, and re-layouts: 3.29 us -> 0.01 us
    pallas_call x4 -> x3, Pallas kernels: 4.72 us -> 2.11 us  [the longest x1 1.83 us: local(): call(first_kernel, outs, [HBM] * 10, scratch)]
  transfers between devices with their start and end apart: 1 -> 0, of which waited for: 1 -> 0; matrix products, arithmetic and copies ran while one was open for 0% -> 0% of each run, Pallas kernels for 2% -> 0%
where the time goes in v5:
time: 74.4 us; the launch traced here: 74.1 us
  blocking collectives  70.2 us (94%)
  Pallas kernels  3.24 us (4%)
    all_to_all x4, blocking collectives, exchange(): return lax.all_to_all(x, 'inst', 0, 0, axis_index_groups=groups, tiled=True)  61.9 us
    all_to_all x1, blocking collectives, local(): shares = lax.all_to_all(terms, 'tp', 0, 0, tiled=True)  8.38 us
    pallas_call x1, Pallas kernels, local(): call(first_kernel, outs, [HBM] * 10, scratch)  1.83 us

profile of v5, /device:TPU:1, one launch (start us, length us, event | category | flops | bytes accessed | tf_op | source)
XLA Modules:
  0.0 74.1 jit_solution(13210371575562479664)
XLA Ops:
  0.0 0.0 copy-start
  0.0 1.8 %shard_map.109 = (bf16[8,48,128]{2,1,0:T(8,128)(2,1)S(1)}, f32[40,128]{1,0:T(8,128)S(1)}, f32[40,128]{1,0:T(8,128)S(1)}, f32[40,128]{1,0:T(8,128)S(1)}, f32[128,...) custom-call(s32[2]{0:T(128)} %ctx_hbm.1, s32[2,4]{1,0:T(2,128)} %blocks_hbm.1, ...), custom_call_target="tpu_custom_call" | custom-call | tf_op jit(solution)/shard_map/pallas_call | solution.py:312
  1.8 15.1 %all_to_all.25.in_ref = bf16[8,48,128]{2,1,0:T(8,128)(2,1)S(1)} all-to-all(bf16[8,48,128]{2,1,0:T(8,128)(2,1)S(1)} %get-tuple-element.13), channel_id=1, replica_groups={{0,64,128,192,256,320,384,448},{4,68,132,196,260,324,388,452},{8,72,136..., dimensions={0} | all-to-all | bytes 196608 | tf_op jit(solution)/shard_map/all_to_all | solution.py:277
  16.9 0.1 shard_map.110
  17.1 22.5 %all_to_all.26.in_ref = bf16[16,48,128]{2,1,0:T(8,128)(2,1)S(1)} all-to-all(bf16[16,48,128]{2,1,0:T(8,128)(2,1)S(1)} %shard_map.110), channel_id=1, replica_groups={{0,4,8,12,16,20,24,28,32,36,40,44,48,52,56,60},{64,68,72,76,80,84,88,92..., dimensions={0} | all-to-all | bytes 393216 | tf_op jit(solution)/shard_map/all_to_all | solution.py:277
  39.6 0.4 shard_map.111
  40.0 13.0 %all_to_all.27.in_ref = bf16[16,48,128]{2,1,0:T(8,128)(2,1)S(1)} all-to-all(bf16[16,48,128]{2,1,0:T(8,128)(2,1)S(1)} %shard_map.111), channel_id=1, replica_groups={{0,4,8,12,16,20,24,28,32,36,40,44,48,52,56,60},{64,68,72,76,80,84,88,92..., dimensions={0} | all-to-all | bytes 393216 | tf_op jit(solution)/shard_map/all_to_all | solution.py:277
  53.0 0.1 shard_map.112
  53.2 11.3 %all_to_all.28.in_ref = bf16[8,48,128]{2,1,0:T(8,128)(2,1)S(1)} all-to-all(bf16[8,48,128]{2,1,0:T(8,128)(2,1)S(1)} %shard_map.112), channel_id=1, replica_groups={{0,64,128,192,256,320,384,448},{4,68,132,196,260,324,388,452},{8,72,136..., dimensions={0} | all-to-all | bytes 196608 | tf_op jit(solution)/shard_map/all_to_all | solution.py:277
  64.4 0.0 copy-done
  64.4 0.7 shard_map.113
  65.1 8.4 %all_to_all.29 = f32[4,8,640]{2,1,0:T(8,128)S(1)} all-to-all(f32[4,8,640]{2,1,0:T(8,128)S(1)} %shard_map.113), channel_id=1, replica_groups=mesh['inst'=128,'tp'=4] {'tp'}, dimensions={0} | all-to-all | bytes 163840 | tf_op jit(solution)/shard_map/all_to_all | solution.py:330
  73.5 0.6 convert_element_type.8
  (1 shorter events, 0.0 us)
Async XLA Ops:
  0.0 64.4 %copy-start = (bf16[640,2560]{1,0:T(8,128)(2,1)S(1)}, bf16[640,2560]{1,0:T(8,128)(2,1)}, u32[]{:S(2)}) copy-start(bf16[640,2560]{1,0:T(8,128)(2,1)} %w_ref.1) | copy-start | bytes 9830404

commit v6 on v5

--- a/solution.py
+++ b/solution.py
@@ -14,11 +14,12 @@
 STEPS = 4
 TILE = ROWS * STEPS
 QROWS = GROUP * TILE
-MSG = 48
+PARTS = GROUP * ROWS + 1
+MSG = PARTS * HEAD
 LOW = -1e30
 PARTS_M = 3
 PARTS_L = 2
-PER_HEAD = PARTS_M + PARTS_L
+PIECES = PARTS_M + PARTS_L
 SCALE = 1.0 / math.sqrt(HEAD)
 F32 = jnp.float32
 BF16 = jnp.bfloat16
@@ -56,6 +57,22 @@
 
 def tile_iota(dim):
     return lax.broadcasted_iota(jnp.int32, (TILE, HEAD), dim)
+
+
+def upper():
+    return tile_iota(0) >= STEPS
+
+
+def by_request(side, apart):
+    both = jnp.concatenate([side] * ROWS, axis=0)
+    return jnp.where(upper(), pltpu.roll(both, HEAD - apart, axis=1), both)
+
+
+def joined(message, h):
+    at = h * ROWS * HEAD
+    return jnp.concatenate(
+        [message[:, at + r * HEAD : at + (r + 1) * HEAD] for r in range(ROWS)], axis=0
+    )
 
 
 def per_head(tile):
@@ -132,16 +149,17 @@
 
     for copy in [copies[0], *copies[3:5]]:
         copy.wait()
-    rows = head_rows(q_ref)
-    q = rows.astype(BF16)
+    q = head_rows(q_ref).astype(BF16)
     res_len, block_len = k_ref.shape[1], lk_ref.shape[1]
-    side = jnp.zeros((TILE, HEAD), F32)
+    side = jnp.zeros((STEPS, HEAD), F32)
     for r in range(ROWS):
         for i in range(blocks_ref.shape[1]):
             fill = jnp.clip(ctx_ref[r] - res_len - i * block_len, 0, block_len)
-            hit = (request == r) & (lane == blocks_ref[r, i])
+            hit = lane[:STEPS] == r * lk_ref.shape[0] + blocks_ref[r, i]
             side = jnp.where(hit, fill.astype(F32), side)
-    message = jnp.concatenate([rows, side], axis=0).astype(BF16)
+    steps = [q_ref[r].astype(F32) for r in range(ROWS)]
+    tiles = [steps[r][:, h * HEAD : (h + 1) * HEAD] for h in range(GROUP) for r in range(ROWS)]
+    message = jnp.concatenate([*tiles, side], axis=1).astype(BF16)
     for i in range(lines):
         out_ref[i] = message
 
@@ -179,17 +197,19 @@
 
 
 def place(pick_ref, in_ref, out_ref, place_of):
-    held = [in_ref[i].astype(F32) for i in range(in_ref.shape[0])]
+    held = []
+    for i in range(in_ref.shape[0]):
+        message = in_ref[i].astype(F32)
+        side = jnp.concatenate([message[:, MSG - HEAD :]] * ROWS, axis=0)
+        held.append([*(joined(message, h) for h in range(GROUP)), side])
     for o in range(out_ref.shape[0]):
-        tiles = [jnp.zeros((TILE, HEAD), F32)] * (MSG // TILE)
+        tiles = [jnp.zeros((TILE, HEAD), F32)] * (GROUP + 1)
         for i, message in enumerate(held):
             at = place_of(i, o)
             mine = jnp.broadcast_to(pick_ref[at : at + 1], (TILE, HEAD)) > 0.5
-            tiles = [
-                jnp.where(mine, message[t * TILE : (t + 1) * TILE], tile)
-                for t, tile in enumerate(tiles)
-            ]
-        out_ref[o] = jnp.concatenate(tiles, axis=0).astype(BF16)
+            tiles = [jnp.where(mine, m, tile) for m, tile in zip(message, tiles)]
+        halves = [t[r * STEPS : (r + 1) * STEPS] for t in tiles[:GROUP] for r in range(ROWS)]
+        out_ref[o] = jnp.concatenate([*halves, tiles[GROUP][:STEPS]], axis=1).astype(BF16)
 
 
 def place_out_kernel(pick_ref, in_ref, out_ref):
@@ -218,8 +238,8 @@
 
 def lent_kernel(in_ref, k_ref, v_ref, out_ref):
     message = merged(in_ref)
-    q = message[:QROWS].astype(BF16)
-    fills = message[QROWS:]
+    q = jnp.concatenate([joined(message, h) for h in range(GROUP)], axis=0).astype(BF16)
+    fills = by_request(message[:, MSG - HEAD :], k_ref.shape[0])
     block_len = k_ref.shape[1]
     k = k_ref[...].reshape(-1, HEAD)
     v = v_ref[...].reshape(-1, HEAD)
@@ -238,25 +258,28 @@
         span = slice(h * TILE, (h + 1) * TILE)
         values = pieces(top[span], PARTS_M) + pieces(total[span], PARTS_L)
         for i, value in enumerate(values):
-            side = jnp.where(tile_iota(1) == h * PER_HEAD + i, value, side)
-    reply = jnp.concatenate([acc, side], axis=0).astype(BF16)
+            side = jnp.where(tile_iota(1) == h * ROWS * PIECES + i, value, side)
+    side = side[:STEPS] + pltpu.roll(side, PIECES, axis=1)[STEPS:]
+    tiles = [acc[i * STEPS : (i + 1) * STEPS] for i in range(GROUP * ROWS)]
+    reply = jnp.concatenate([*tiles, side], axis=1).astype(BF16)
     for i in range(out_ref.shape[0]):
         out_ref[i] = reply
 
 
 def project_kernel(in_ref, o_ref, m_ref, l_ref, w_ref, out_ref):
     reply = merged(in_ref)
-    side = reply[QROWS:]
+    side = by_request(reply[:, MSG - HEAD :], PIECES)
     heads = []
     for h in range(GROUP):
         span = slice(h * TILE, (h + 1) * TILE)
-        cols = [side[:, h * PER_HEAD + i : h * PER_HEAD + i + 1] for i in range(PER_HEAD)]
+        first = h * ROWS * PIECES
+        cols = [side[:, first + i : first + i + 1] for i in range(PIECES)]
         lent_top = cols[0] + cols[1] + cols[2]
         lent_total = cols[3] + cols[4]
         top = jnp.maximum(m_ref[span], lent_top)
         a = jnp.exp(m_ref[span] - top)
         b = jnp.exp(lent_top - top) * lent_total
-        mixed = (a * o_ref[span] + b * reply[span]) / (a * l_ref[span] + b)
+        mixed = (a * o_ref[span] + b * joined(reply, h)) / (a * l_ref[span] + b)
         heads.append(mixed.astype(BF16))
     attended = jnp.concatenate(heads, axis=1)
     width = out_ref.shape[2]
@@ -290,7 +313,7 @@
         out_proj,
     ):
         def slots(n):
-            return jax.ShapeDtypeStruct((n, MSG, HEAD), BF16)
+            return jax.ShapeDtypeStruct((n, STEPS, MSG), BF16)
 
         def like(x, space=pltpu.VMEM):
             return space(x.shape, x.dtype)

time: 74.4 us -> 73.6 us (0.989)
  blocking collectives: 70.2 us -> 69.2 us
    all_to_all x4, blocking collectives: 61.9 us -> 60.8 us  [exchange(): return lax.all_to_all(x, 'inst', 0, 0, axis_index_groups=groups, tiled=True)]
where the time goes in v6:
time: 73.6 us; the launch traced here: 73.3 us
  blocking collectives  69.2 us (94%)
  Pallas kernels  3.44 us (5%)
    all_to_all x4, blocking collectives, exchange(): return lax.all_to_all(x, 'inst', 0, 0, axis_index_groups=groups, tiled=True)  60.8 us
    all_to_all x1, blocking collectives, local(): shares = lax.all_to_all(terms, 'tp', 0, 0, tiled=True)  8.38 us
    pallas_call x1, Pallas kernels, local(): call(first_kernel, outs, [HBM] * 10, scratch)  1.83 us

profile of v6, /device:TPU:1, one launch (start us, length us, event | category | flops | bytes accessed | tf_op | source)
XLA Modules:
  0.0 73.3 jit_solution(1689875622342172225)
XLA Ops:
  0.0 0.0 copy-start
  0.0 1.8 %shard_map.109 = (bf16[8,4,1408]{2,1,0:T(4,128)(2,1)S(1)}, f32[40,128]{1,0:T(8,128)S(1)}, f32[40,128]{1,0:T(8,128)S(1)}, f32[40,128]{1,0:T(8,128)S(1)}, f32[128,...) custom-call(s32[2]{0:T(128)} %ctx_hbm.1, s32[2,4]{1,0:T(2,128)} %blocks_hbm.1, ...), custom_call_target="tpu_custom_call" | custom-call | tf_op jit(solution)/shard_map/pallas_call | solution.py:335
  1.8 15.0 %all_to_all.25.in_ref = bf16[8,4,1408]{2,1,0:T(4,128)(2,1)S(1)} all-to-all(bf16[8,4,1408]{2,1,0:T(4,128)(2,1)S(1)} %get-tuple-element.13), channel_id=1, replica_groups={{0,64,128,192,256,320,384,448},{4,68,132,196,260,324,388,452},{8,72,136..., dimensions={0} | all-to-all | bytes 180224 | tf_op jit(solution)/shard_map/all_to_all | solution.py:300
  16.9 0.2 shard_map.110
  17.1 22.1 %all_to_all.26.in_ref = bf16[16,4,1408]{2,1,0:T(4,128)(2,1)S(1)} all-to-all(bf16[16,4,1408]{2,1,0:T(4,128)(2,1)S(1)} %shard_map.110), channel_id=1, replica_groups={{0,4,8,12,16,20,24,28,32,36,40,44,48,52,56,60},{64,68,72,76,80,84,88,92..., dimensions={0} | all-to-all | bytes 360448 | tf_op jit(solution)/shard_map/all_to_all | solution.py:300
  39.2 0.5 shard_map.111
  39.6 12.6 %all_to_all.27.in_ref = bf16[16,4,1408]{2,1,0:T(4,128)(2,1)S(1)} all-to-all(bf16[16,4,1408]{2,1,0:T(4,128)(2,1)S(1)} %shard_map.111), channel_id=1, replica_groups={{0,4,8,12,16,20,24,28,32,36,40,44,48,52,56,60},{64,68,72,76,80,84,88,92..., dimensions={0} | all-to-all | bytes 360448 | tf_op jit(solution)/shard_map/all_to_all | solution.py:300
  52.3 0.2 shard_map.112
  52.5 11.1 %all_to_all.28.in_ref = bf16[8,4,1408]{2,1,0:T(4,128)(2,1)S(1)} all-to-all(bf16[8,4,1408]{2,1,0:T(4,128)(2,1)S(1)} %shard_map.112), channel_id=1, replica_groups={{0,64,128,192,256,320,384,448},{4,68,132,196,260,324,388,452},{8,72,136..., dimensions={0} | all-to-all | bytes 180224 | tf_op jit(solution)/shard_map/all_to_all | solution.py:300
  63.5 0.0 copy-done
  63.5 0.8 %shard_map.113 = f32[4,8,640]{2,1,0:T(8,128)S(1)} custom-call(bf16[8,4,1408]{2,1,0:T(4,128)(2,1)S(1)} %all_to_all.28.in_ref, f32[40,128]{1,0:T(8,128)S(1)} %get-tuple-element.16.o_ref, f32[40,128]{1,0:T(8,128)S(1)} %get-tuple-element.17.m_ref, f32[40,128]{1,0:T(8,128)S(1)} %get-tuple-element.18.l_ref, bf16[640,2560]{1,0:T(8,128)(2,1)S(1)} %copy-done), custom_call_target="tpu_custom_call" | custom-call | tf_op jit(solution)/shard_map/pallas_call | solution.py:348
  64.3 8.4 %all_to_all.29 = f32[4,8,640]{2,1,0:T(8,128)S(1)} all-to-all(f32[4,8,640]{2,1,0:T(8,128)S(1)} %shard_map.113), channel_id=1, replica_groups=mesh['inst'=128,'tp'=4] {'tp'}, dimensions={0} | all-to-all | bytes 163840 | tf_op jit(solution)/shard_map/all_to_all | solution.py:353
  72.7 0.6 convert_element_type.8
  (1 shorter events, 0.0 us)
Async XLA Ops:
  0.0 63.5 %copy-start = (bf16[640,2560]{1,0:T(8,128)(2,1)S(1)}, bf16[640,2560]{1,0:T(8,128)(2,1)}, u32[]{:S(2)}) copy-start(bf16[640,2560]{1,0:T(8,128)(2,1)} %w_ref.1) | copy-start | bytes 9830404

commit v7 on v6

--- a/solution.py
+++ b/solution.py
@@ -21,6 +21,9 @@
 PARTS_L = 2
 PIECES = PARTS_M + PARTS_L
 SCALE = 1.0 / math.sqrt(HEAD)
+LINE = (0, 4, 2, 6, 1, 5, 3, 7)
+ROW = (*range(0, 16, 2), *range(1, 16, 2))
+SHARD = (0, 2, 1, 3)
 F32 = jnp.float32
 BF16 = jnp.bfloat16
 
@@ -141,11 +144,11 @@
     me = lax.axis_index("inst")
     row, col = me // per_row, me % per_row
     target = jnp.zeros((lines, HEAD), jnp.int32)
-    for y in range(lines):
-        here = lax.broadcasted_iota(jnp.int32, (lines, HEAD), 0) == y
+    for i, y in enumerate(LINE):
+        here = lax.broadcasted_iota(jnp.int32, (lines, HEAD), 0) == i
         target = jnp.where(here, lender_ref[y * per_row + col] - row * per_row, target)
-    for s in range(per_row):
-        pick_ref[s * lines : (s + 1) * lines] = jnp.where(target == s, 1.0, 0.0)
+    for s, c in enumerate(ROW):
+        pick_ref[s * lines : (s + 1) * lines] = jnp.where(target == c, 1.0, 0.0)
 
     for copy in [copies[0], *copies[3:5]]:
         copy.wait()
@@ -283,18 +286,17 @@
         heads.append(mixed.astype(BF16))
     attended = jnp.concatenate(heads, axis=1)
     width = out_ref.shape[2]
-    for i in range(out_ref.shape[0]):
+    for i, x in enumerate(SHARD):
         out_ref[i] = jnp.dot(
-            attended, w_ref[:, i * width : (i + 1) * width], preferred_element_type=F32
+            attended, w_ref[:, x * width : (x + 1) * width], preferred_element_type=F32
         )
 
 
 def solution(mesh):
     insts, shards = mesh.shape["inst"], mesh.shape["tp"]
-    per_row = 16
-    lines = insts // per_row
-    along_y = [[y * per_row + c for y in range(lines)] for c in range(per_row)]
-    along_row = [[y * per_row + c for c in range(per_row)] for y in range(lines)]
+    per_row, lines = len(ROW), len(LINE)
+    along_y = [[y * per_row + c for y in LINE] for c in range(per_row)]
+    along_row = [[y * per_row + c for c in ROW] for y in range(lines)]
 
     def exchange(x, groups):
         return lax.all_to_all(x, "inst", 0, 0, axis_index_groups=groups, tiled=True)
@@ -350,7 +352,9 @@
             jax.ShapeDtypeStruct((shards, TILE, width), F32),
             [VMEM] * 5,
         )(returned, *home, out_proj)
-        shares = lax.all_to_all(terms, "tp", 0, 0, tiled=True)
+        shares = lax.all_to_all(
+            terms, "tp", 0, 0, axis_index_groups=[list(SHARD)], tiled=True
+        )
         return jnp.sum(shares, axis=0).astype(BF16).reshape(ROWS, STEPS, width)
 
     in_specs = (

time: 73.6 us -> 70.6 us (0.959)
  the two profiles are of different devices: /device:TPU:1 before, /device:TPU:64 now
where the time goes in v7:
time: 70.6 us; the launch traced here: 70.3 us
  blocking collectives  66.2 us (94%)
  Pallas kernels  3.44 us (5%)
    all_to_all x4, blocking collectives, exchange(): return lax.all_to_all(x, 'inst', 0, 0, axis_index_groups=groups, tiled=True)  56.6 us
    all_to_all x1, blocking collectives, local(): lax.all_to_all(terms, 'tp', 0, 0, axis_index_groups=[list(SHARD)], tiled=...  9.59 us
    pallas_call x1, Pallas kernels, local(): call(first_kernel, outs, [HBM] * 10, scratch)  1.83 us

profile of v7, /device:TPU:64, one launch (start us, length us, event | category | flops | bytes accessed | tf_op | source)
XLA Modules:
  0.0 70.3 jit_solution(8388366143045545973)
XLA Ops:
  0.0 0.0 copy-start
  0.0 1.8 %shard_map.109 = (bf16[8,4,1408]{2,1,0:T(4,128)(2,1)S(1)}, f32[40,128]{1,0:T(8,128)S(1)}, f32[40,128]{1,0:T(8,128)S(1)}, f32[40,128]{1,0:T(8,128)S(1)}, f32[128,...) custom-call(s32[2]{0:T(128)} %ctx_hbm.1, s32[2,4]{1,0:T(2,128)} %blocks_hbm.1, ...), custom_call_target="tpu_custom_call" | custom-call | tf_op jit(solution)/shard_map/pallas_call | solution.py:337
  1.8 14.7 %all_to_all.25.in_ref = bf16[8,4,1408]{2,1,0:T(4,128)(2,1)S(1)} all-to-all(bf16[8,4,1408]{2,1,0:T(4,128)(2,1)S(1)} %get-tuple-element.13), channel_id=1, replica_groups={{0,256,128,384,64,320,192,448},{4,260,132,388,68,324,196,452},{8,264,13..., dimensions={0} | all-to-all | bytes 180224 | tf_op jit(solution)/shard_map/all_to_all | solution.py:302
  16.5 0.2 shard_map.110
  16.7 19.0 %all_to_all.26.in_ref = bf16[16,4,1408]{2,1,0:T(4,128)(2,1)S(1)} all-to-all(bf16[16,4,1408]{2,1,0:T(4,128)(2,1)S(1)} %shard_map.110), channel_id=1, replica_groups={{0,8,16,24,32,40,48,56,4,12,20,28,36,44,52,60},{64,72,80,88,96,104,112,..., dimensions={0} | all-to-all | bytes 360448 | tf_op jit(solution)/shard_map/all_to_all | solution.py:302
  35.7 0.5 shard_map.111
  36.2 12.6 %all_to_all.27.in_ref = bf16[16,4,1408]{2,1,0:T(4,128)(2,1)S(1)} all-to-all(bf16[16,4,1408]{2,1,0:T(4,128)(2,1)S(1)} %shard_map.111), channel_id=1, replica_groups={{0,8,16,24,32,40,48,56,4,12,20,28,36,44,52,60},{64,72,80,88,96,104,112,..., dimensions={0} | all-to-all | bytes 360448 | tf_op jit(solution)/shard_map/all_to_all | solution.py:302
  48.9 0.2 shard_map.112
  49.1 10.3 %all_to_all.28.in_ref = bf16[8,4,1408]{2,1,0:T(4,128)(2,1)S(1)} all-to-all(bf16[8,4,1408]{2,1,0:T(4,128)(2,1)S(1)} %shard_map.112), channel_id=1, replica_groups={{0,256,128,384,64,320,192,448},{4,260,132,388,68,324,196,452},{8,264,13..., dimensions={0} | all-to-all | bytes 180224 | tf_op jit(solution)/shard_map/all_to_all | solution.py:302
  59.3 0.0 copy-done
  59.3 0.8 %shard_map.113 = f32[4,8,640]{2,1,0:T(8,128)S(1)} custom-call(bf16[8,4,1408]{2,1,0:T(4,128)(2,1)S(1)} %all_to_all.28.in_ref, f32[40,128]{1,0:T(8,128)S(1)} %get-tuple-element.16.o_ref, f32[40,128]{1,0:T(8,128)S(1)} %get-tuple-element.17.m_ref, f32[40,128]{1,0:T(8,128)S(1)} %get-tuple-element.18.l_ref, bf16[640,2560]{1,0:T(8,128)(2,1)S(1)} %copy-done), custom_call_target="tpu_custom_call" | custom-call | tf_op jit(solution)/shard_map/pallas_call | solution.py:350
  60.1 9.6 %all_to_all.29 = f32[4,8,640]{2,1,0:T(8,128)S(1)} all-to-all(f32[4,8,640]{2,1,0:T(8,128)S(1)} %shard_map.113), channel_id=1, replica_groups={{0,2,1,3},{4,6,5,7},{8,10,9,11},{12,14,13,15},{16,18,17,19},{20,22,21,2..., dimensions={0} | all-to-all | bytes 163840 | tf_op jit(solution)/shard_map/all_to_all | solution.py:355
  69.7 0.6 convert_element_type.8
  (1 shorter events, 0.0 us)
Async XLA Ops:
  0.0 59.3 %copy-start = (bf16[640,2560]{1,0:T(8,128)(2,1)S(1)}, bf16[640,2560]{1,0:T(8,128)(2,1)}, u32[]{:S(2)}) copy-start(bf16[640,2560]{1,0:T(8,128)(2,1)} %w_ref.1) | copy-start | bytes 9830404

commit v8 on v7

--- a/solution.py
+++ b/solution.py
@@ -22,7 +22,7 @@
 PIECES = PARTS_M + PARTS_L
 SCALE = 1.0 / math.sqrt(HEAD)
 LINE = (0, 4, 2, 6, 1, 5, 3, 7)
-ROW = (*range(0, 16, 2), *range(1, 16, 2))
+ROW = (0, 2, 4, 6, 9, 11, 13, 15, 1, 3, 5, 7, 8, 10, 12, 14)
 SHARD = (0, 2, 1, 3)
 F32 = jnp.float32
 BF16 = jnp.bfloat16

time: 70.6 us -> 70 us (level)
  no operation moved by 1% of the time
where the time goes in v8:
time: 70 us; the launch traced here: 69.8 us
  blocking collectives  65.7 us (94%)
  Pallas kernels  3.44 us (5%)
    all_to_all x4, blocking collectives, exchange(): return lax.all_to_all(x, 'inst', 0, 0, axis_index_groups=groups, tiled=True)  56.1 us
    all_to_all x1, blocking collectives, local(): lax.all_to_all(terms, 'tp', 0, 0, axis_index_groups=[list(SHARD)], tiled=...  9.59 us
    pallas_call x1, Pallas kernels, local(): call(first_kernel, outs, [HBM] * 10, scratch)  1.83 us

profile of v8, /device:TPU:64, one launch (start us, length us, event | category | flops | bytes accessed | tf_op | source)
XLA Modules:
  0.0 69.8 jit_solution(2470086048300579175)
XLA Ops:
  0.0 0.0 copy-start
  0.0 1.8 %shard_map.109 = (bf16[8,4,1408]{2,1,0:T(4,128)(2,1)S(1)}, f32[40,128]{1,0:T(8,128)S(1)}, f32[40,128]{1,0:T(8,128)S(1)}, f32[40,128]{1,0:T(8,128)S(1)}, f32[128,...) custom-call(s32[2]{0:T(128)} %ctx_hbm.1, s32[2,4]{1,0:T(2,128)} %blocks_hbm.1, ...), custom_call_target="tpu_custom_call" | custom-call | tf_op jit(solution)/shard_map/pallas_call | solution.py:337
  1.8 14.7 %all_to_all.25.in_ref = bf16[8,4,1408]{2,1,0:T(4,128)(2,1)S(1)} all-to-all(bf16[8,4,1408]{2,1,0:T(4,128)(2,1)S(1)} %get-tuple-element.13), channel_id=1, replica_groups={{0,256,128,384,64,320,192,448},{4,260,132,388,68,324,196,452},{8,264,13..., dimensions={0} | all-to-all | bytes 180224 | tf_op jit(solution)/shard_map/all_to_all | solution.py:302
  16.5 0.2 shard_map.110
  16.7 18.3 %all_to_all.26.in_ref = bf16[16,4,1408]{2,1,0:T(4,128)(2,1)S(1)} all-to-all(bf16[16,4,1408]{2,1,0:T(4,128)(2,1)S(1)} %shard_map.110), channel_id=1, replica_groups={{0,8,16,24,36,44,52,60,4,12,20,28,32,40,48,56},{64,72,80,88,100,108,116..., dimensions={0} | all-to-all | bytes 360448 | tf_op jit(solution)/shard_map/all_to_all | solution.py:302
  35.0 0.5 shard_map.111
  35.5 12.6 %all_to_all.27.in_ref = bf16[16,4,1408]{2,1,0:T(4,128)(2,1)S(1)} all-to-all(bf16[16,4,1408]{2,1,0:T(4,128)(2,1)S(1)} %shard_map.111), channel_id=1, replica_groups={{0,8,16,24,36,44,52,60,4,12,20,28,32,40,48,56},{64,72,80,88,100,108,116..., dimensions={0} | all-to-all | bytes 360448 | tf_op jit(solution)/shard_map/all_to_all | solution.py:302
  48.1 0.2 shard_map.112
  48.3 10.5 %all_to_all.28.in_ref = bf16[8,4,1408]{2,1,0:T(4,128)(2,1)S(1)} all-to-all(bf16[8,4,1408]{2,1,0:T(4,128)(2,1)S(1)} %shard_map.112), channel_id=1, replica_groups={{0,256,128,384,64,320,192,448},{4,260,132,388,68,324,196,452},{8,264,13..., dimensions={0} | all-to-all | bytes 180224 | tf_op jit(solution)/shard_map/all_to_all | solution.py:302
  58.8 0.0 copy-done
  58.8 0.8 %shard_map.113 = f32[4,8,640]{2,1,0:T(8,128)S(1)} custom-call(bf16[8,4,1408]{2,1,0:T(4,128)(2,1)S(1)} %all_to_all.28.in_ref, f32[40,128]{1,0:T(8,128)S(1)} %get-tuple-element.16.o_ref, f32[40,128]{1,0:T(8,128)S(1)} %get-tuple-element.17.m_ref, f32[40,128]{1,0:T(8,128)S(1)} %get-tuple-element.18.l_ref, bf16[640,2560]{1,0:T(8,128)(2,1)S(1)} %copy-done), custom_call_target="tpu_custom_call" | custom-call | tf_op jit(solution)/shard_map/pallas_call | solution.py:350
  59.6 9.6 %all_to_all.29 = f32[4,8,640]{2,1,0:T(8,128)S(1)} all-to-all(f32[4,8,640]{2,1,0:T(8,128)S(1)} %shard_map.113), channel_id=1, replica_groups={{0,2,1,3},{4,6,5,7},{8,10,9,11},{12,14,13,15},{16,18,17,19},{20,22,21,2..., dimensions={0} | all-to-all | bytes 163840 | tf_op jit(solution)/shard_map/all_to_all | solution.py:355
  69.2 0.6 convert_element_type.8
  (1 shorter events, 0.0 us)
Async XLA Ops:
  0.0 58.8 %copy-start = (bf16[640,2560]{1,0:T(8,128)(2,1)S(1)}, bf16[640,2560]{1,0:T(8,128)(2,1)}, u32[]{:S(2)}) copy-start(bf16[640,2560]{1,0:T(8,128)(2,1)} %w_ref.1) | copy-start | bytes 9830404

commit v9 on v8

--- a/solution.py
+++ b/solution.py
@@ -22,8 +22,8 @@
 PIECES = PARTS_M + PARTS_L
 SCALE = 1.0 / math.sqrt(HEAD)
 LINE = (0, 4, 2, 6, 1, 5, 3, 7)
-ROW = (0, 2, 4, 6, 9, 11, 13, 15, 1, 3, 5, 7, 8, 10, 12, 14)
-SHARD = (0, 2, 1, 3)
+ROW = (0, 2, 9, 11, 4, 6, 13, 15, 1, 3, 8, 10, 5, 7, 12, 14)
+SHARD = (0, 1, 3, 2)
 F32 = jnp.float32
 BF16 = jnp.bfloat16
 

time: 70 us -> 69.6 us (level)
  the two profiles are of different devices: /device:TPU:64 before, /device:TPU:1 now
where the time goes in v9:
time: 69.6 us; the launch traced here: 68.6 us
  blocking collectives  64.5 us (93%)
  Pallas kernels  3.44 us (5%)
    all_to_all x4, blocking collectives, exchange(): return lax.all_to_all(x, 'inst', 0, 0, axis_index_groups=groups, tiled=True)  56.4 us
    all_to_all x1, blocking collectives, local(): lax.all_to_all(terms, 'tp', 0, 0, axis_index_groups=[list(SHARD)], tiled=...  8.16 us
    pallas_call x1, Pallas kernels, local(): call(first_kernel, outs, [HBM] * 10, scratch)  1.83 us

profile of v9, /device:TPU:1, one launch (start us, length us, event | category | flops | bytes accessed | tf_op | source)
XLA Modules:
  0.0 68.6 jit_solution(15331514665369376292)
XLA Ops:
  0.0 0.0 copy-start
  0.0 1.8 %shard_map.109 = (bf16[8,4,1408]{2,1,0:T(4,128)(2,1)S(1)}, f32[40,128]{1,0:T(8,128)S(1)}, f32[40,128]{1,0:T(8,128)S(1)}, f32[40,128]{1,0:T(8,128)S(1)}, f32[128,...) custom-call(s32[2]{0:T(128)} %ctx_hbm.1, s32[2,4]{1,0:T(2,128)} %blocks_hbm.1, ...), custom_call_target="tpu_custom_call" | custom-call | tf_op jit(solution)/shard_map/pallas_call | solution.py:337
  1.8 14.1 %all_to_all.25.in_ref = bf16[8,4,1408]{2,1,0:T(4,128)(2,1)S(1)} all-to-all(bf16[8,4,1408]{2,1,0:T(4,128)(2,1)S(1)} %get-tuple-element.13), channel_id=1, replica_groups={{0,256,128,384,64,320,192,448},{4,260,132,388,68,324,196,452},{8,264,13..., dimensions={0} | all-to-all | bytes 180224 | tf_op jit(solution)/shard_map/all_to_all | solution.py:302
  15.9 0.2 shard_map.110
  16.1 20.8 %all_to_all.26.in_ref = bf16[16,4,1408]{2,1,0:T(4,128)(2,1)S(1)} all-to-all(bf16[16,4,1408]{2,1,0:T(4,128)(2,1)S(1)} %shard_map.110), channel_id=1, replica_groups={{0,8,36,44,16,24,52,60,4,12,32,40,20,28,48,56},{64,72,100,108,80,88,116..., dimensions={0} | all-to-all | bytes 360448 | tf_op jit(solution)/shard_map/all_to_all | solution.py:302
  36.9 0.5 shard_map.111
  37.4 12.4 %all_to_all.27.in_ref = bf16[16,4,1408]{2,1,0:T(4,128)(2,1)S(1)} all-to-all(bf16[16,4,1408]{2,1,0:T(4,128)(2,1)S(1)} %shard_map.111), channel_id=1, replica_groups={{0,8,36,44,16,24,52,60,4,12,32,40,20,28,48,56},{64,72,100,108,80,88,116..., dimensions={0} | all-to-all | bytes 360448 | tf_op jit(solution)/shard_map/all_to_all | solution.py:302
  49.8 0.2 shard_map.112
  50.0 9.1 %all_to_all.28.in_ref = bf16[8,4,1408]{2,1,0:T(4,128)(2,1)S(1)} all-to-all(bf16[8,4,1408]{2,1,0:T(4,128)(2,1)S(1)} %shard_map.112), channel_id=1, replica_groups={{0,256,128,384,64,320,192,448},{4,260,132,388,68,324,196,452},{8,264,13..., dimensions={0} | all-to-all | bytes 180224 | tf_op jit(solution)/shard_map/all_to_all | solution.py:302
  59.1 0.0 copy-done
  59.1 0.8 %shard_map.113 = f32[4,8,640]{2,1,0:T(8,128)S(1)} custom-call(bf16[8,4,1408]{2,1,0:T(4,128)(2,1)S(1)} %all_to_all.28.in_ref, f32[40,128]{1,0:T(8,128)S(1)} %get-tuple-element.16.o_ref, f32[40,128]{1,0:T(8,128)S(1)} %get-tuple-element.17.m_ref, f32[40,128]{1,0:T(8,128)S(1)} %get-tuple-element.18.l_ref, bf16[640,2560]{1,0:T(8,128)(2,1)S(1)} %copy-done), custom_call_target="tpu_custom_call" | custom-call | tf_op jit(solution)/shard_map/pallas_call | solution.py:350
  59.9 8.2 %all_to_all.29 = f32[4,8,640]{2,1,0:T(8,128)S(1)} all-to-all(f32[4,8,640]{2,1,0:T(8,128)S(1)} %shard_map.113), channel_id=1, replica_groups={{0,1,3,2},{4,5,7,6},{8,9,11,10},{12,13,15,14},{16,17,19,18},{20,21,23,2..., dimensions={0} | all-to-all | bytes 163840 | tf_op jit(solution)/shard_map/all_to_all | solution.py:355
  68.0 0.6 convert_element_type.8
  (1 shorter events, 0.0 us)
Async XLA Ops:
  0.0 59.1 %copy-start = (bf16[640,2560]{1,0:T(8,128)(2,1)S(1)}, bf16[640,2560]{1,0:T(8,128)(2,1)}, u32[]{:S(2)}) copy-start(bf16[640,2560]{1,0:T(8,128)(2,1)} %w_ref.1) | copy-start | bytes 9830404

commit v10 on v9

--- a/solution.py
+++ b/solution.py
@@ -286,10 +286,9 @@
         heads.append(mixed.astype(BF16))
     attended = jnp.concatenate(heads, axis=1)
     width = out_ref.shape[2]
+    terms = jnp.dot(attended, w_ref[...], preferred_element_type=F32)
     for i, x in enumerate(SHARD):
-        out_ref[i] = jnp.dot(
-            attended, w_ref[:, x * width : (x + 1) * width], preferred_element_type=F32
-        )
+        out_ref[i] = terms[:, x * width : (x + 1) * width]
 
 
 def solution(mesh):

time: 69.6 us -> 69.6 us (level)
  no operation moved by 1% of the time
where the time goes in v10:
time: 69.6 us; the launch traced here: 68.6 us
  blocking collectives  64.5 us (93%)
  Pallas kernels  3.42 us (5%)
    all_to_all x4, blocking collectives, exchange(): return lax.all_to_all(x, 'inst', 0, 0, axis_index_groups=groups, tiled=True)  56.4 us
    all_to_all x1, blocking collectives, local(): lax.all_to_all(terms, 'tp', 0, 0, axis_index_groups=[list(SHARD)], tiled=...  8.15 us
    pallas_call x1, Pallas kernels, local(): call(first_kernel, outs, [HBM] * 10, scratch)  1.83 us

profile of v10, /device:TPU:1, one launch (start us, length us, event | category | flops | bytes accessed | tf_op | source)
XLA Modules:
  0.0 68.6 jit_solution(2980664637947722914)
XLA Ops:
  0.0 0.0 copy-start
  0.0 1.8 %shard_map.109 = (bf16[8,4,1408]{2,1,0:T(4,128)(2,1)S(1)}, f32[40,128]{1,0:T(8,128)S(1)}, f32[40,128]{1,0:T(8,128)S(1)}, f32[40,128]{1,0:T(8,128)S(1)}, f32[128,...) custom-call(s32[2]{0:T(128)} %ctx_hbm.1, s32[2,4]{1,0:T(2,128)} %blocks_hbm.1, ...), custom_call_target="tpu_custom_call" | custom-call | tf_op jit(solution)/shard_map/pallas_call | solution.py:336
  1.8 14.1 %all_to_all.25.in_ref = bf16[8,4,1408]{2,1,0:T(4,128)(2,1)S(1)} all-to-all(bf16[8,4,1408]{2,1,0:T(4,128)(2,1)S(1)} %get-tuple-element.13), channel_id=1, replica_groups={{0,256,128,384,64,320,192,448},{4,260,132,388,68,324,196,452},{8,264,13..., dimensions={0} | all-to-all | bytes 180224 | tf_op jit(solution)/shard_map/all_to_all | solution.py:301
  15.9 0.2 shard_map.110
  16.1 20.8 %all_to_all.26.in_ref = bf16[16,4,1408]{2,1,0:T(4,128)(2,1)S(1)} all-to-all(bf16[16,4,1408]{2,1,0:T(4,128)(2,1)S(1)} %shard_map.110), channel_id=1, replica_groups={{0,8,36,44,16,24,52,60,4,12,32,40,20,28,48,56},{64,72,100,108,80,88,116..., dimensions={0} | all-to-all | bytes 360448 | tf_op jit(solution)/shard_map/all_to_all | solution.py:301
  36.9 0.5 shard_map.111
  37.4 12.4 %all_to_all.27.in_ref = bf16[16,4,1408]{2,1,0:T(4,128)(2,1)S(1)} all-to-all(bf16[16,4,1408]{2,1,0:T(4,128)(2,1)S(1)} %shard_map.111), channel_id=1, replica_groups={{0,8,36,44,16,24,52,60,4,12,32,40,20,28,48,56},{64,72,100,108,80,88,116..., dimensions={0} | all-to-all | bytes 360448 | tf_op jit(solution)/shard_map/all_to_all | solution.py:301
  49.8 0.2 shard_map.112
  50.0 9.1 %all_to_all.28.in_ref = bf16[8,4,1408]{2,1,0:T(4,128)(2,1)S(1)} all-to-all(bf16[8,4,1408]{2,1,0:T(4,128)(2,1)S(1)} %shard_map.112), channel_id=1, replica_groups={{0,256,128,384,64,320,192,448},{4,260,132,388,68,324,196,452},{8,264,13..., dimensions={0} | all-to-all | bytes 180224 | tf_op jit(solution)/shard_map/all_to_all | solution.py:301
  59.1 0.0 copy-done
  59.1 0.7 %shard_map.113 = f32[4,8,640]{2,1,0:T(8,128)S(1)} custom-call(bf16[8,4,1408]{2,1,0:T(4,128)(2,1)S(1)} %all_to_all.28.in_ref, f32[40,128]{1,0:T(8,128)S(1)} %get-tuple-element.16.o_ref, f32[40,128]{1,0:T(8,128)S(1)} %get-tuple-element.17.m_ref, f32[40,128]{1,0:T(8,128)S(1)} %get-tuple-element.18.l_ref, bf16[640,2560]{1,0:T(8,128)(2,1)S(1)} %copy-done), custom_call_target="tpu_custom_call" | custom-call | tf_op jit(solution)/shard_map/pallas_call | solution.py:349
  59.8 8.2 %all_to_all.29 = f32[4,8,640]{2,1,0:T(8,128)S(1)} all-to-all(f32[4,8,640]{2,1,0:T(8,128)S(1)} %shard_map.113), channel_id=1, replica_groups={{0,1,3,2},{4,5,7,6},{8,9,11,10},{12,13,15,14},{16,17,19,18},{20,21,23,2..., dimensions={0} | all-to-all | bytes 163840 | tf_op jit(solution)/shard_map/all_to_all | solution.py:354
  68.0 0.6 convert_element_type.8
  (1 shorter events, 0.0 us)
Async XLA Ops:
  0.0 59.1 %copy-start = (bf16[640,2560]{1,0:T(8,128)(2,1)S(1)}, bf16[640,2560]{1,0:T(8,128)(2,1)}, u32[]{:S(2)}) copy-start(bf16[640,2560]{1,0:T(8,128)(2,1)} %w_ref.1) | copy-start | bytes 9830404
